TPU v7x, 256 devices: a whole 4x4x8 slice. The times are simulated.
256 devices in a mesh: tiles: 64 (over z, x, core), pair: 4 (over y).
Axes of the slice: x: 4, y: 4, z: 8, core: 2. Of those that a mesh axis runs over, the one named last changes fastest.
Arguments:
- t2: bfloat16 [2048, 16, 4096], P('tiles', None, 'pair'), may hold values from -6 to 6
- v_plus: bfloat16 [64, 64, 16, 2048], P('tiles'), may hold values from -0.1875 to 0.1875
- v_minus: bfloat16 [64, 64, 16, 2048], P('tiles'), may hold values from -0.1875 to 0.1875
- partner: int32 [4096], P('pair'), may hold values from 0 to 1023, as said below
- win_tile: int32 [64, 64], replicated, may hold values from 0 to 2047, as said below
- win_count: int32 [64], replicated, may hold values from 48 to 64, as said below
Outputs:
- ladder: bfloat16 [4096, 131072], P('pair', 'tiles')
Inputs may be any that keep to these rules, and one draw needn't show every extreme that they name: `partner`: each block of 1024 entries is a permutation of 0 to 1023, and blocks 2h and 2h + 1 are inverse to each other. `win_tile`: the live entries of one owner's list name distinct tiles; at most 2 of them lie among one index of tiles' 32 tiles (tiles k * 32 to (k + 1) * 32 - 1), and some owner takes exactly 2 from one index in every draw. Entries past the live count name tiles too. `win_count`: some owner has exactly 64 live slots.
All inputs are finite; a program needn't handle non-finite values.
Results may differ from a plain program's by a relative error of at most 0.0052.
Values may be sent and summed in bfloat16 or wider, within the bound.
No kernel may reach another device: no remote copies, remote signals or barrier semaphores. Data moves between devices by JAX's collectives and lax.ppermute only.
A program may use at most 128 MiB of HBM per device.

v0:
```python
import jax
import jax.numpy as jnp
from jax import lax
from jax.sharding import PartitionSpec as P


def partner_2(x, axis, stride):
    return lax.ppermute(x, axis, [(i, i ^ 1 << stride) for i in range(lax.axis_size(axis))])


def route_plan(win_tile, win_count, per_source):
    window_slots = win_tile.shape[1]
    sources = win_tile // per_source
    offsets = win_tile % per_source
    positions = jnp.arange(window_slots)
    living = positions[None, :] < win_count[:, None]
    earlier = positions[None, None, :] < positions[None, :, None]
    same_source = (sources[:, :, None] == sources[:, None, :]) & living[:, None, :] & earlier
    ranked = jnp.sum(same_source, axis=2)
    return (sources, offsets, ranked, living)


def pack_sends(payload, sources, offsets, ranked, living, owner_index, capacity):
    per_source = payload.shape[0]
    owner_count = sources.shape[0]
    hits = (living & (sources == owner_index)).astype(jnp.float32)
    rank_hot = (ranked[:, :, None] == jnp.arange(capacity)[None, None, :]).astype(jnp.float32)
    tile_hot = (offsets[:, :, None] == jnp.arange(per_source)[None, None, :]).astype(jnp.float32)
    select = jnp.einsum("ow,owc,owt->oct", hits, rank_hot, tile_hot).astype(jnp.bfloat16)
    select = select.reshape(owner_count * capacity, per_source)
    outgoing = jnp.dot(select, payload, preferred_element_type=jnp.float32).astype(jnp.bfloat16)
    return outgoing.reshape(owner_count, capacity, payload.shape[1])


def unpack_window(received, source_row, rank_row, living_row, capacity):
    owner_count = received.shape[0]
    flat = received.reshape(owner_count * capacity, received.shape[2])
    target = source_row * capacity + rank_row
    picking = living_row[:, None] & (target[:, None] == jnp.arange(owner_count * capacity)[None, :])
    return jnp.dot(picking.astype(jnp.bfloat16), flat, preferred_element_type=jnp.float32).astype(
        jnp.bfloat16
    )


def body(t2, v_plus, v_minus, partner, win_tile, win_count):
    per_source, tile_width, pair_rows = t2.shape
    owner_count = lax.axis_size("tiles")
    window_slots = win_tile.shape[1]
    capacity = max(2, (window_slots + owner_count - 1) // owner_count)
    owner_index = lax.axis_index("tiles")
    sources, offsets, ranked, living = route_plan(win_tile, win_count, per_source)
    source_row = lax.dynamic_index_in_dim(sources, owner_index, 0, keepdims=False)
    rank_row = lax.dynamic_index_in_dim(ranked, owner_index, 0, keepdims=False)
    living_row = lax.dynamic_index_in_dim(living, owner_index, 0, keepdims=False)
    plus_slab = v_plus[0]
    minus_slab = v_minus[0]
    outgoing = pack_sends(
        t2.reshape(per_source, tile_width * pair_rows),
        sources,
        offsets,
        ranked,
        living,
        owner_index,
        capacity,
    )
    received = lax.all_to_all(outgoing, "tiles", split_axis=0, concat_axis=0, tiled=True)
    own_window = unpack_window(received, source_row, rank_row, living_row, capacity).reshape(
        window_slots, tile_width, pair_rows
    )
    mirrored = partner_2(own_window, "pair", 0)
    own_values = own_window.astype(jnp.float32)
    mirror_values = jnp.take(mirrored, partner, axis=2).astype(jnp.float32)
    wplus = (own_values + mirror_values).astype(jnp.bfloat16)
    wminus = (own_values - mirror_values).astype(jnp.bfloat16)
    contract = (((0, 1), (0, 1)), ((), ()))
    summed = lax.dot_general(wplus, plus_slab, contract, preferred_element_type=jnp.float32)
    summed = summed + lax.dot_general(
        wminus, minus_slab, contract, preferred_element_type=jnp.float32
    )
    ladder = (0.5 * summed).astype(jnp.bfloat16)
    return ladder


def solution(mesh):
    placed = (
        P("tiles", None, "pair"),
        P("tiles", None, None, None),
        P("tiles", None, None, None),
        P("pair"),
        P(),
        P(),
    )
    return jax.shard_map(
        body, mesh=mesh, in_specs=placed, out_specs=P("pair", "tiles"), check_vma=False
    )
```

profile of v0, /device:TPU:28, one launch (start us, length us, event | category | flops | bytes accessed | tf_op | source)
XLA Modules:
  0.0 224.5 jit_solution(7592839659230307842)
XLA Ops:
  0.0 0.8 add_select_fusion.1
  0.8 1.8 copy.21
  2.6 0.9 iota_compare_fusion.4
  3.5 1.9 convert_reduce_fusion
  5.3 0.4 convolution_convert_fusion.2
  5.7 3.3 %convolution_convert_fusion = bf16[128,16384]{1,0:T(8,128)(2,1)} fusion(bf16[128,32]{1,0:T(8,128)(2,1)S(1)} %bitcast.50, bf16[32,16384]{1,0:T(8,128)(2,1)S(1)} %bitcast.44), kind=kOutput, calls=%fused_computation.1 | convolution fusion | flops 136314880 | bytes 5251072 | tf_op jit(solution)/shard_map/dot_general | solution.py:31
  9.0 7.7 %reshape.78 = bf16[64,2,16384]{2,1,0:T(2,128)(2,1)} reshape(bf16[128,16384]{1,0:T(8,128)(2,1)} %convolution_convert_fusion) | data formatting | bytes 8388608 | tf_op jit(solution)/shard_map/reshape | solution.py:32
  16.6 12.2 %all-to-all-start = ((bf16[64,2,16384]{2,1,0:T(2,128)(2,1)}), bf16[64,2,16384]{2,1,0:T(2,128)(2,1)}, u32[]{:S(2)}, u32[]{:S(2)}) async-start(bf16[64,2,16384]{2,1,0:T(2,128)(2,1)} %reshape.78), calls=%async_computation | async-start | bytes 8388608 | tf_op jit(solution)/shard_map/all_to_all | solution.py:66
  28.9 96.1 %all-to-all-done = bf16[64,2,16384]{2,1,0:T(2,128)(2,1)} async-done(((bf16[64,2,16384]{2,1,0:T(2,128)(2,1)}), bf16[64,2,16384]{2,1,0:T(2,128)(2,1)}, u32[]{:S(2)}, u32[]{:S(2)}) %all-to-all-start) | async-done | bytes 4194336 | tf_op jit(solution)/shard_map/all_to_all | solution.py:66
  125.0 7.2 %reshape.79 = bf16[128,16384]{1,0:T(8,128)(2,1)} reshape(bf16[64,2,16384]{2,1,0:T(2,128)(2,1)} %all-to-all-done) | data formatting | bytes 8388608 | tf_op jit(solution)/shard_map/reshape | solution.py:37
  132.1 0.0 copy-start
  132.1 3.0 %convolution_convert_fusion.1 = bf16[64,16384]{1,0:T(8,128)(2,1)S(1)} fusion(bf16[128,16384]{1,0:T(8,128)(2,1)} %reshape.79, s32[64]{0:T(128)S(1)} %fusion.21, pred[64]{0:T(512)(128)(4,1)S(1)} %dynamic-slice_bitcast_fusion), kind=kOutput, calls=%fused_computation.2 | convolution fusion | flops 269500416 | bytes 6291776 | tf_op jit(solution)/shard_map/dot_general | solution.py:40
  135.1 1.2 copy.23
  136.3 1.0 collective-permute-start
  137.3 0.0 copy-done
  137.4 44.7 %collective-permute-done = bf16[64,16,1024]{2,1,0:T(8,128)(2,1)} collective-permute-done((bf16[64,16,1024]{2,1,0:T(8,128)(2,1)S(1)}, bf16[64,16,1024]{2,1,0:T(8,128)(2,1)}, u32[]{:S(2)}, u32[]{:S(2)}) %collective-permute-start) | collective-permute-done | bytes 2097184 | tf_op jit(solution)/shard_map/ppermute | solution.py:8
  182.0 8.2 %copy.19 = bf16[64,16,1024]{0,1,2:T(8,128)(2,1)} copy(bf16[64,16,1024]{2,1,0:T(8,128)(2,1)} %collective-permute-done) | data formatting | bytes 4194304 | tf_op jit(solution)/shard_map/ppermute | solution.py:8
  190.2 10.5 %gather_fusion = bf16[1024,64,16]{1,2,0:T(8,128)(2,1)} fusion(bf16[64,16,1024]{0,1,2:T(8,128)(2,1)} %copy.19, s32[1024]{0:T(1024)S(1)} %fusion.18), kind=kCustom, calls=%fused_computation | custom fusion | bytes 4198400 | tf_op jit(solution)/shard_map/jit(_take)/gather | solution.py:72
  200.7 6.8 %copy.20 = bf16[64,16,1024]{2,1,0:T(8,128)(2,1)} copy(bf16[64,16,1024]{0,1,2:T(8,128)(2,1)} %bitcast.39) | data formatting | bytes 4194304 | tf_op jit(solution)/shard_map/jit(_take)/gather | solution.py:72
  207.6 2.8 %copy.24 = bf16[8,8,16,1024]{3,1,2,0:T(8,128)(2,1)S(1)} copy(bf16[8,8,16,1024]{3,2,1,0:T(8,128)(2,1)} %bitcast.40) | data formatting | bytes 4194304
  210.4 1.0 fusion.3
  211.3 0.0 copy-start.1
  211.4 1.2 copy.26
  212.6 1.2 copy.25
  213.8 0.0 copy-done.1
  213.8 0.0 copy-start.2
  213.8 4.6 %fusion.5 = f32[1024,2048,1]{1,0,2:T(8,128)S(1)} fusion(bf16[64,16,1024]{2,1,0:T(8,128)(2,1)S(1)} %bitcast.47, bf16[1,64,16,2048]{3,2,1,0:T(8,128)(2,1)S(1)} %copy-done.1), kind=kOutput, calls=%fused_computation.11 | convolution fusion | flops 4294967296 | bytes 14680064 | tf_op jit(solution)/shard_map/dot_general | solution.py:76
  218.4 0.0 copy-done.2
  218.4 6.1 %fusion.1 = bf16[1024,2048]{1,0:T(8,128)(2,1)} fusion(f32[1024,2048,1]{1,0,2:T(8,128)S(1)} %fusion.5, bf16[64,16,1024]{2,1,0:T(8,128)(2,1)S(1)} %bitcast.46, bf16[1,64,16,2048]{3,2,1,0:T(8,128)(2,1)S(1)} %copy-done.2), kind=kOutput, calls=%fused_computation.5 | convolution fusion | flops 4301258752 | bytes 18874368 | tf_op jit(solution)/shard_map/dot_general | solution.py:77
  (6 shorter events, 0.1 us)
Async XLA Ops:
  16.6 108.3 %all-to-all-start = ((bf16[64,2,16384]{2,1,0:T(2,128)(2,1)}), bf16[64,2,16384]{2,1,0:T(2,128)(2,1)}, u32[]{:S(2)}, u32[]{:S(2)}) async-start(bf16[64,2,16384]{2,1,0:T(2,128)(2,1)} %reshape.78), calls=%async_computation | async-start | bytes 8388608 | tf_op jit(solution)/shard_map/all_to_all | solution.py:66
  132.1 5.2 %copy-start = (s32[1024]{0:T(1024)S(1)}, s32[1024]{0:T(1024)}, u32[]{:S(2)}) copy-start(s32[1024]{0:T(1024)} %param.9) | copy-start | bytes 12292
  136.3 45.7 %collective-permute-start = (bf16[64,16,1024]{2,1,0:T(8,128)(2,1)S(1)}, bf16[64,16,1024]{2,1,0:T(8,128)(2,1)}, u32[]{:S(2)}, u32[]{:S(2)}) collective-permute-start(bf16[64,16,1024]{2,1,0:T(8,128)(2,1)S(1)} %bitcast.45), channel_id=1, source_target_pairs={{0,1},{1,0},{2,3},{3,2},{4,5},{5,4},{6,7},{7,6},{8,9},{9,8},{10,11... | collective-permute-start | bytes 6291464 | tf_op jit(solution)/shard_map/ppermute | solution.py:8
  211.3 2.4 %copy-start.1 = (bf16[1,64,16,2048]{3,2,1,0:T(8,128)(2,1)S(1)}, bf16[1,64,16,2048]{3,2,1,0:T(8,128)(2,1)}, u32[]{:S(2)}) copy-start(bf16[1,64,16,2048]{3,2,1,0:T(8,128)(2,1)} %param.7) | copy-start | bytes 12582916
  213.8 4.6 %copy-start.2 = (bf16[1,64,16,2048]{3,2,1,0:T(8,128)(2,1)S(1)}, bf16[1,64,16,2048]{3,2,1,0:T(8,128)(2,1)}, u32[]{:S(2)}) copy-start(bf16[1,64,16,2048]{3,2,1,0:T(8,128)(2,1)} %param.8) | copy-start | bytes 12582916
where the time goes:
time: 226 us; the launch traced here: 225 us
  waiting for transfers between devices  141 us (62%)
  local copies, waits for them, and re-layouts  48.6 us (22%)
  matrix products  17.3 us (8%)
  starting transfers between devices  13.2 us (6%)
  other arithmetic  4.52 us (2%)
    all_to_all x1, waiting for transfers between devices, body(): lax.all_to_all(outgoing, 'tiles', split_axis=0, concat_axis=0, tiled=True)  96.1 us
    ppermute x1, waiting for transfers between devices, partner_2(): lax.ppermute(x, axis, [(i, i ^ 1 << stride) for i in range(lax.axis_size(...  44.7 us
    gather x2, local copies, waits for them, and re-layouts, body(): mirror_values = jnp.take(mirrored, partner, axis=2).astype(jnp.float32)  17.3 us
    all_to_all x1, starting transfers between devices, body(): lax.all_to_all(outgoing, 'tiles', split_axis=0, concat_axis=0, tiled=True)  12.2 us
    unnamed x13, local copies, waits for them, and re-layouts  8.27 us
    ppermute x1, local copies, waits for them, and re-layouts, partner_2(): lax.ppermute(x, axis, [(i, i ^ 1 << stride) for i in range(lax.axis_size(...  8.17 us
    reshape x1, local copies, waits for them, and re-layouts, pack_sends(): return outgoing.reshape(owner_count, capacity, payload.shape[1])  7.66 us
    reshape x1, local copies, waits for them, and re-layouts, unpack_window(): flat = received.reshape(owner_count * capacity, received.shape[2])  7.17 us
  transfers between devices with their start and end apart: 2, of which 2 were waited for; matrix products, arithmetic and copies ran while one was open for 0% of the time, Pallas kernels for 0%

commit v1 on v0

v1 whole, which is shorter than its diff:
```python
import functools

import jax
import jax.numpy as jnp
from jax import lax
from jax.experimental import pallas as pl
from jax.experimental.pallas import tpu as pltpu
from jax.sharding import PartitionSpec as P

CHUNKS = (640, 256, 128)
VMEM_LIMIT = 20 * 1024 * 1024


def mirror_pair(x):
    return lax.ppermute(x, "pair", [(i, i ^ 1) for i in range(lax.axis_size("pair"))])


def whole(count):
    return [pl.BlockSpec(memory_space=pltpu.VMEM)] * count


def scalars():
    return [pl.BlockSpec(memory_space=pltpu.SMEM)]


def params():
    return pltpu.CompilerParams(vmem_limit_bytes=VMEM_LIMIT)


def pack_kernel(table_ref, tiles_ref, out_ref):
    for k in range(out_ref.shape[0]):
        out_ref[k] = tiles_ref[table_ref[k]]


def pack(table, tiles):
    count = table.shape[0]
    return pl.pallas_call(
        pack_kernel,
        out_shape=jax.ShapeDtypeStruct((count,) + tiles.shape[1:], tiles.dtype),
        in_specs=scalars() + whole(1),
        out_specs=whole(1)[0],
        compiler_params=params(),
    )(table, tiles)


def window_kernel(where_ref, received_ref, out_ref):
    for w in range(out_ref.shape[0]):
        place = where_ref[w]
        tile = received_ref[jnp.maximum(place, 0)]
        out_ref[w] = jnp.where(place >= 0, tile, jnp.zeros_like(tile))


def unpack(where, received):
    return pl.pallas_call(
        window_kernel,
        out_shape=jax.ShapeDtypeStruct(where.shape + received.shape[1:], received.dtype),
        in_specs=scalars() + whole(1),
        out_specs=whole(1)[0],
        compiler_params=params(),
    )(where, received)


def ladder_kernel(first, block, *refs):
    own_ref, mirror_ref, restore_ref, plus_ref, minus_ref = refs[:5]
    base_ref = None if first else refs[5]
    out_ref = refs[5 if first else 6]
    slots, tile_width, width = own_ref.shape
    depth = slots * tile_width
    own = own_ref[...].reshape(depth, width).astype(jnp.float32)
    mirrored = mirror_ref[...].reshape(depth, width).astype(jnp.float32)
    plus = (own + mirrored).astype(jnp.bfloat16).T
    minus = (own - mirrored).astype(jnp.bfloat16).T
    restore = restore_ref[...]
    for begin in range(0, out_ref.shape[1], block):
        across = slice(begin, begin + block)
        total = jnp.dot(
            plus,
            plus_ref[:, :, across].reshape(depth, block),
            preferred_element_type=jnp.float32,
        )
        total = total + jnp.dot(
            minus,
            minus_ref[:, :, across].reshape(depth, block),
            preferred_element_type=jnp.float32,
        )
        ladder = jnp.dot(
            restore, (0.5 * total).astype(jnp.bfloat16), preferred_element_type=jnp.float32
        )
        if not first:
            ladder = ladder + base_ref[:, across].astype(jnp.float32)
        out_ref[:, across] = ladder.astype(out_ref.dtype)


def add_rows(own, mirrored, restore, plus_slab, minus_slab, base, block=512):
    slots, tile_width, width = own.shape
    columns = plus_slab.shape[2]
    rows = restore.shape[0]
    first = base is None
    return pl.pallas_call(
        functools.partial(ladder_kernel, first, block),
        out_shape=jax.ShapeDtypeStruct((rows, columns), jnp.bfloat16),
        in_specs=whole(5 if first else 6),
        out_specs=whole(1)[0],
        compiler_params=params(),
        cost_estimate=pl.CostEstimate(
            flops=4 * slots * tile_width * width * columns + 2 * rows * width * columns,
            bytes_accessed=4 * slots * tile_width * columns + 4 * rows * columns,
            transcendentals=0,
        ),
    )(own, mirrored, restore, plus_slab, minus_slab, *([] if first else [base]))


def route_plan(win_tile, win_count, me):
    slots = win_tile.shape[1]
    position = jnp.arange(slots)
    sources = win_tile >> 5
    mine = (sources == me) & (position[None, :] < win_count[:, None])
    coded = position[None, :] * 32 + (win_tile & 31)
    first = jnp.min(jnp.where(mine, coded, 1 << 20), axis=1) & 31
    last = jnp.maximum(jnp.max(jnp.where(mine, coded, -1), axis=1), 0) & 31
    send = jnp.stack([first, last], axis=1).reshape(-1)
    own = lax.dynamic_index_in_dim(sources, me, 0, keepdims=False)
    living = position < lax.dynamic_index_in_dim(win_count, me, 0, keepdims=False)
    earlier = (
        (own[:, None] == own[None, :])
        & living[None, :]
        & (position[None, :] < position[:, None])
    )
    rank = jnp.any(earlier, axis=1).astype(jnp.int32)
    return send, jnp.where(living, own * 2 + rank, -1)


def after(value, *others):
    return lax.optimization_barrier((value,) + others)[0]


def body(t2, v_plus, v_minus, partner, win_tile, win_count):
    tiles, tile_width, rows = t2.shape
    me = lax.axis_index("tiles")
    odd = lax.axis_index("pair") % 2 == 1
    index = jnp.arange(rows)
    order = jnp.where(odd, partner, index)
    send, where = route_plan(win_tile, win_count, me)
    flat = t2.reshape(tiles * tile_width, rows)
    ladder = None
    begin = 0
    windows = []
    for width in CHUNKS:
        select = (order[:, None] == index[None, begin : begin + width]).astype(jnp.bfloat16)
        chunk = jnp.dot(flat, select, preferred_element_type=jnp.float32).astype(jnp.bfloat16)
        outgoing = pack(send, chunk.reshape(tiles, tile_width, width))
        if windows:
            outgoing = after(outgoing, received)
        received = lax.all_to_all(outgoing, "tiles", 0, 0, tiled=True)
        windows.append((received, begin, width))
        begin += width
    for received, begin, width in windows:
        own = unpack(where, received)
        mirrored = mirror_pair(own)
        restore = (order[:, None] == index[None, begin : begin + width]).astype(jnp.bfloat16)
        ladder = add_rows(own, mirrored, restore, v_plus[0], v_minus[0], ladder)
    return ladder


def solution(mesh):
    placed = (
        P("tiles", None, "pair"),
        P("tiles", None, None, None),
        P("tiles", None, None, None),
        P("pair"),
        P(),
        P(),
    )
    return jax.shard_map(
        body, mesh=mesh, in_specs=placed, out_specs=P("pair", "tiles"), check_vma=False
    )
```

time: 226 us -> 159 us (0.70)
  waiting for transfers between devices: 141 us -> 81.1 us
  local copies, waits for them, and re-layouts: 48.6 us -> 15.6 us
  Pallas kernels: 0 us -> 28.4 us
  matrix products: 17.3 us -> 2.55 us
  starting transfers between devices: 13.2 us -> 26 us
    ppermute x1 -> x3, waiting for transfers between devices: 44.7 us -> 0.12 us  [mirror_pair(): lax.ppermute(x, 'pair', [(i, i ^ 1) for i in range(lax.axis_size('pair'))])]
    pallas_call x0 -> x9, Pallas kernels: none -> 28.4 us  [the longest x3 19.6 us: add_rows(): pl.pallas_call(functools.partial(ladder_kernel, first, block), out_shape=...]
    gather x2 -> x0, local copies, waits for them, and re-layouts: 17.3 us -> none  [body(): mirror_values = jnp.take(mirrored, partner, axis=2).astype(jnp.float32)]
    all_to_all x1 -> x3, waiting for transfers between devices: 96.1 us -> 81 us  [body(): received = lax.all_to_all(outgoing, 'tiles', 0, 0, tiled=True)]
    dot_general x5 -> x3, matrix products: 17.3 us -> 2.55 us  [body(): jnp.dot(flat, select, preferred_element_type=jnp.float32)]
    reshape x2 -> x1, local copies, waits for them, and re-layouts: 14.8 us -> 0.14 us  [route_plan(): send = jnp.stack([first, last], axis=1).reshape(-1)]
    all_to_all x1 -> x3, starting transfers between devices: 12.2 us -> 23.4 us  [body(): received = lax.all_to_all(outgoing, 'tiles', 0, 0, tiled=True)]
    ppermute x1 -> x0, local copies, waits for them, and re-layouts: 8.17 us -> none  [partner_2(): lax.ppermute(x, axis, [(i, i ^ 1 << stride) for i in range(lax.axis_size(...]
  transfers between devices with their start and end apart: 2 -> 6, of which waited for: 2 -> 3; matrix products, arithmetic and copies ran while one was open for 0% -> 3% of each run, Pallas kernels for 0% -> 14%
where the time goes in v1:
time: 159 us; the launch traced here: 158 us
  waiting for transfers between devices  81.1 us (51%)
  Pallas kernels  28.4 us (18%)
  starting transfers between devices  26 us (16%)
  local copies, waits for them, and re-layouts  15.6 us (10%)
  other arithmetic  3.93 us (2%)
  matrix products  2.55 us (2%)
    all_to_all x3, waiting for transfers between devices, body(): received = lax.all_to_all(outgoing, 'tiles', 0, 0, tiled=True)  81 us
    all_to_all x3, starting transfers between devices, body(): received = lax.all_to_all(outgoing, 'tiles', 0, 0, tiled=True)  23.4 us
    pallas_call x3, Pallas kernels, add_rows(): pl.pallas_call(functools.partial(ladder_kernel, first, block), out_shape=...  19.6 us
    unnamed x22, local copies, waits for them, and re-layouts  14.5 us
    pallas_call x3, Pallas kernels, unpack(): pl.pallas_call(window_kernel, out_shape=jax.ShapeDtypeStruct(where.shape...  4.91 us
    pallas_call x3, Pallas kernels, pack(): pl.pallas_call(pack_kernel, out_shape=jax.ShapeDtypeStruct((count,) + til...  3.84 us
  transfers between devices with their start and end apart: 6, of which 3 were waited for; matrix products, arithmetic and copies ran while one was open for 3% of the time, Pallas kernels for 14%

profile of v1, /device:TPU:28, one launch (start us, length us, event | category | flops | bytes accessed | tf_op | source)
XLA Modules:
  0.0 157.7 jit_solution(848346980693190772)
XLA Ops:
  0.0 1.0 select_reduce_fusion.1
  1.3 0.7 iota_select_fusion
  2.0 1.1 fusion.2
  3.1 0.8 shard_map.66
  3.9 1.5 copy-done.7
  5.4 12.2 %all-to-all-start = ((bf16[128,16,640]{2,1,0:T(8,128)(2,1)}), bf16[128,16,640]{2,1,0:T(8,128)(2,1)}, u32[]{:S(2)}, u32[]{:S(2)}) async-start(bf16[128,16,640]{2,1,0:T(8,128)(2,1)} %copy-done.7), calls=%async_computation | async-start | bytes 5242880 | tf_op jit(solution)/shard_map/all_to_all | solution.py:154
  17.6 0.7 fusion.7
  18.5 1.6 %shard_map.65 = bf16[128,16,256]{2,1,0:T(8,128)(2,1)} custom-call(s32[128]{0:T(128)S(1)} %reshape.54.table_ref, bf16[32,16,256]{2,1,0:T(8,128)(2,1)S(1)} %bitcast.34), custom_call_target="tpu_custom_call" | custom-call | tf_op jit(solution)/shard_map/pallas_call | solution.py:37
  20.1 59.9 %all-to-all-done.received_ref = bf16[128,16,640]{2,1,0:T(8,128)(2,1)} async-done(((bf16[128,16,640]{2,1,0:T(8,128)(2,1)}), bf16[128,16,640]{2,1,0:T(8,128)(2,1)}, u32[]{:S(2)}, u32[]{:S(2)}) %all-to-all-start) | async-done | bytes 2621472 | tf_op jit(solution)/shard_map/all_to_all | solution.py:154
  80.0 5.4 %all-to-all-start.1 = ((bf16[128,16,256]{2,1,0:T(8,128)(2,1)}), bf16[128,16,256]{2,1,0:T(8,128)(2,1)S(1)}, u32[]{:S(2)}, u32[]{:S(2)}) async-start(bf16[128,16,256]{2,1,0:T(8,128)(2,1)} %shard_map.65), calls=%async_computation.1 | async-start | bytes 2097152 | tf_op jit(solution)/shard_map/all_to_all | solution.py:154
  85.4 0.6 dynamic_slice.8
  86.0 0.6 iota_compare_fusion.2
  86.9 0.7 add_select_fusion.where_ref
  87.6 3.0 %shard_map.69.refs_0_ = bf16[64,16,640]{2,1,0:T(8,128)(2,1)} custom-call(s32[64]{0:T(128)S(1)} %add_select_fusion.where_ref, bf16[128,16,640]{2,1,0:T(8,128)(2,1)} %all-to-all-done.received_ref), custom_call_target="tpu_custom_call" | custom-call | tf_op jit(solution)/shard_map/pallas_call | solution.py:54
  90.7 0.7 fusion.8
  91.5 1.5 shard_map.64
  93.2 21.1 %all-to-all-done.1.received_ref = bf16[128,16,256]{2,1,0:T(8,128)(2,1)S(1)} async-done(((bf16[128,16,256]{2,1,0:T(8,128)(2,1)}), bf16[128,16,256]{2,1,0:T(8,128)(2,1)S(1)}, u32[]{:S(2)}, u32[]{:S(2)}) %all-to-all-start.1) | async-done | bytes 1048608 | tf_op jit(solution)/shard_map/all_to_all | solution.py:154
  114.2 5.8 %all-to-all-start.2 = ((bf16[128,16,128]{2,1,0:T(8,128)(2,1)}), bf16[128,16,128]{2,1,0:T(8,128)(2,1)}, u32[]{:S(2)}, u32[]{:S(2)}) async-start(bf16[128,16,128]{2,1,0:T(8,128)(2,1)} %shard_map.64), calls=%async_computation.2 | async-start | bytes 1048576 | tf_op jit(solution)/shard_map/all_to_all | solution.py:154
  120.3 0.3 compare_convert_fusion.refs_2_
  120.6 0.7 shard_map.68.refs_0_
  121.3 0.3 collective-permute-start.1
  121.7 2.2 %copy-done.1 = bf16[1,64,16,2048]{3,2,1,0:T(8,128)(2,1)S(1)} copy-done((bf16[1,64,16,2048]{3,2,1,0:T(8,128)(2,1)S(1)}, bf16[1,64,16,2048]{3,2,1,0:T(8,128)(2,1)}, u32[]{:S(2)}) %copy-start.1) | copy-done | bytes 4194328
  123.9 2.2 %copy-done.4 = bf16[1,64,16,2048]{3,2,1,0:T(8,128)(2,1)S(1)} copy-done((bf16[1,64,16,2048]{3,2,1,0:T(8,128)(2,1)S(1)}, bf16[1,64,16,2048]{3,2,1,0:T(8,128)(2,1)}, u32[]{:S(2)}) %copy-start.4) | copy-done | bytes 4194328
  126.1 10.7 %shard_map.70.refs_5_ = bf16[1024,2048]{1,0:T(8,128)(2,1)S(1)} custom-call(bf16[64,16,640]{2,1,0:T(8,128)(2,1)} %shard_map.69.refs_0_, bf16[64,16,640]{2,1,0:T(8,128)(2,1)} %collective-permute-done.2.refs_1_, bf16[1024,640]{1,0:T(8,128)(2,1)S(1)} %compare_convert_fusion.refs_2_, bf16[64,16,2048]{2,1,0:T(8,128)(2,1)S(1)} %bitcast.28, ...), custom_call_target="tpu_custom_call" | custom-call | flops 8053063680 | bytes 16777216 | tf_op jit(solution)/shard_map/pallas_call | solution.py:99
  136.8 2.0 %copy-done.8 = bf16[1024,2048]{1,0:T(8,128)(2,1)} copy-done((bf16[1024,2048]{1,0:T(8,128)(2,1)}, bf16[1024,2048]{1,0:T(8,128)(2,1)S(1)}, u32[]{:S(2)}) %copy-start.8) | copy-done | bytes 4194328
  138.8 1.2 shard_map.67.refs_0_
  140.0 2.1 %collective-permute-start = (bf16[64,16,128]{2,1,0:T(8,128)(2,1)S(1)}, bf16[64,16,128]{2,1,0:T(8,128)(2,1)S(1)}, u32[]{:S(2)}, u32[]{:S(2)}) collective-permute-start(bf16[64,16,128]{2,1,0:T(8,128)(2,1)S(1)} %shard_map.67.refs_0_), channel_id=1, source_target_pairs={{0,1},{1,0},{2,3},{3,2},{4,5},{5,4},{6,7},{7,6},{8,9},{9,8},{10,11... | collective-permute-start | bytes 786440 | tf_op jit(solution)/shard_map/ppermute | solution.py:15
  142.2 2.2 %copy-done.2 = bf16[1,64,16,2048]{3,2,1,0:T(8,128)(2,1)S(1)} copy-done((bf16[1,64,16,2048]{3,2,1,0:T(8,128)(2,1)S(1)}, bf16[1,64,16,2048]{3,2,1,0:T(8,128)(2,1)}, u32[]{:S(2)}) %copy-start.2) | copy-done | bytes 4194328
  144.4 2.2 %copy-done.5 = bf16[1,64,16,2048]{3,2,1,0:T(8,128)(2,1)S(1)} copy-done((bf16[1,64,16,2048]{3,2,1,0:T(8,128)(2,1)S(1)}, bf16[1,64,16,2048]{3,2,1,0:T(8,128)(2,1)}, u32[]{:S(2)}) %copy-start.5) | copy-done | bytes 4194328
  146.6 2.2 %copy-done.9 = bf16[1024,2048]{1,0:T(8,128)(2,1)S(1)} copy-done((bf16[1024,2048]{1,0:T(8,128)(2,1)S(1)}, bf16[1024,2048]{1,0:T(8,128)(2,1)}, u32[]{:S(2)}) %copy-start.9) | copy-done | bytes 4194328
  148.8 4.0 %shard_map.71.refs_5_ = bf16[1024,2048]{1,0:T(8,128)(2,1)S(1)} custom-call(bf16[64,16,256]{2,1,0:T(8,128)(2,1)S(1)} %shard_map.68.refs_0_, bf16[64,16,256]{2,1,0:T(8,128)(2,1)S(1)} %collective-permute-done.1.refs_1_, bf16[1024,256]{1,0:T(8,128)(2,1)S(1)} %compare_convert_fusion.1.refs_2_, bf16[64,16,2048]{2,1,0:T(8,128)(2,1)S(1)} %bitcast.29, ...), custom_call_target="tpu_custom_call" | custom-call | flops 3221225472 | bytes 16777216 | tf_op jit(solution)/shard_map/pallas_call | solution.py:99
  152.8 4.9 %shard_map.72 = bf16[1024,2048]{1,0:T(8,128)(2,1)} custom-call(bf16[64,16,128]{2,1,0:T(8,128)(2,1)S(1)} %shard_map.67.refs_0_, bf16[64,16,128]{2,1,0:T(8,128)(2,1)S(1)} %collective-permute-done.refs_1_, bf16[1024,128]{1,0:T(8,128)(2,1)S(1)} %compare_convert_fusion.2.refs_2_, bf16[64,16,2048]{2,1,0:T(8,128)(2,1)S(1)} %bitcast.30, ...), custom_call_target="tpu_custom_call" | custom-call | flops 1610612736 | bytes 16777216 | tf_op jit(solution)/shard_map/pallas_call | solution.py:99
  (36 shorter events, 1.3 us)
Async XLA Ops:
  0.0 2.0 %copy-start = (bf16[32,16,1024]{2,1,0:T(8,128)(2,1)S(1)}, bf16[32,16,1024]{2,1,0:T(8,128)(2,1)}, u32[]{:S(2)}) copy-start(bf16[32,16,1024]{2,1,0:T(8,128)(2,1)} %param.6) | copy-start | bytes 3145732
  3.9 1.5 copy-start.7
  5.4 74.6 %all-to-all-start = ((bf16[128,16,640]{2,1,0:T(8,128)(2,1)}), bf16[128,16,640]{2,1,0:T(8,128)(2,1)}, u32[]{:S(2)}, u32[]{:S(2)}) async-start(bf16[128,16,640]{2,1,0:T(8,128)(2,1)} %copy-done.7), calls=%async_computation | async-start | bytes 5242880 | tf_op jit(solution)/shard_map/all_to_all | solution.py:154
  17.6 67.9 %copy-start.10 = (s32[64]{0:T(128)S(1)}, s32[64]{0:T(128)}, u32[]{:S(2)}) copy-start(s32[64]{0:T(128)} %param.11) | copy-start | bytes 772
  80.0 34.2 %all-to-all-start.1 = ((bf16[128,16,256]{2,1,0:T(8,128)(2,1)}), bf16[128,16,256]{2,1,0:T(8,128)(2,1)S(1)}, u32[]{:S(2)}, u32[]{:S(2)}) async-start(bf16[128,16,256]{2,1,0:T(8,128)(2,1)} %shard_map.65), calls=%async_computation.1 | async-start | bytes 2097152 | tf_op jit(solution)/shard_map/all_to_all | solution.py:154
  90.6 31.1 %collective-permute-start.2 = (bf16[64,16,640]{2,1,0:T(8,128)(2,1)}, bf16[64,16,640]{2,1,0:T(8,128)(2,1)}, u32[]{:S(2)}, u32[]{:S(2)}) collective-permute-start(bf16[64,16,640]{2,1,0:T(8,128)(2,1)} %shard_map.69.refs_0_), channel_id=1, source_target_pairs={{0,1},{1,0},{2,3},{3,2},{4,5},{5,4},{6,7},{7,6},{8,9},{9,8},{10,11... | collective-permute-start | bytes 3932168 | tf_op jit(solution)/shard_map/ppermute | solution.py:15
  114.2 24.6 %all-to-all-start.2 = ((bf16[128,16,128]{2,1,0:T(8,128)(2,1)}), bf16[128,16,128]{2,1,0:T(8,128)(2,1)}, u32[]{:S(2)}, u32[]{:S(2)}) async-start(bf16[128,16,128]{2,1,0:T(8,128)(2,1)} %shard_map.64), calls=%async_computation.2 | async-start | bytes 1048576 | tf_op jit(solution)/shard_map/all_to_all | solution.py:154
  121.3 20.9 %collective-permute-start.1 = (bf16[64,16,256]{2,1,0:T(8,128)(2,1)S(1)}, bf16[64,16,256]{2,1,0:T(8,128)(2,1)S(1)}, u32[]{:S(2)}, u32[]{:S(2)}) collective-permute-start(bf16[64,16,256]{2,1,0:T(8,128)(2,1)S(1)} %shard_map.68.refs_0_), channel_id=1, source_target_pairs={{0,1},{1,0},{2,3},{3,2},{4,5},{5,4},{6,7},{7,6},{8,9},{9,8},{10,11... | collective-permute-start | bytes 1572872 | tf_op jit(solution)/shard_map/ppermute | solution.py:15
  121.7 2.2 %copy-start.1 = (bf16[1,64,16,2048]{3,2,1,0:T(8,128)(2,1)S(1)}, bf16[1,64,16,2048]{3,2,1,0:T(8,128)(2,1)}, u32[]{:S(2)}) copy-start(bf16[1,64,16,2048]{3,2,1,0:T(8,128)(2,1)} %param.7) | copy-start | bytes 12582916
  123.9 2.2 %copy-start.4 = (bf16[1,64,16,2048]{3,2,1,0:T(8,128)(2,1)S(1)}, bf16[1,64,16,2048]{3,2,1,0:T(8,128)(2,1)}, u32[]{:S(2)}) copy-start(bf16[1,64,16,2048]{3,2,1,0:T(8,128)(2,1)} %param.8) | copy-start | bytes 12582916
  136.8 2.0 %copy-start.8 = (bf16[1024,2048]{1,0:T(8,128)(2,1)}, bf16[1024,2048]{1,0:T(8,128)(2,1)S(1)}, u32[]{:S(2)}) copy-start(bf16[1024,2048]{1,0:T(8,128)(2,1)S(1)} %shard_map.70.refs_5_) | copy-start | bytes 12582916
  140.0 12.7 %collective-permute-start = (bf16[64,16,128]{2,1,0:T(8,128)(2,1)S(1)}, bf16[64,16,128]{2,1,0:T(8,128)(2,1)S(1)}, u32[]{:S(2)}, u32[]{:S(2)}) collective-permute-start(bf16[64,16,128]{2,1,0:T(8,128)(2,1)S(1)} %shard_map.67.refs_0_), channel_id=1, source_target_pairs={{0,1},{1,0},{2,3},{3,2},{4,5},{5,4},{6,7},{7,6},{8,9},{9,8},{10,11... | collective-permute-start | bytes 786440 | tf_op jit(solution)/shard_map/ppermute | solution.py:15
  142.2 2.2 %copy-start.2 = (bf16[1,64,16,2048]{3,2,1,0:T(8,128)(2,1)S(1)}, bf16[1,64,16,2048]{3,2,1,0:T(8,128)(2,1)}, u32[]{:S(2)}) copy-start(bf16[1,64,16,2048]{3,2,1,0:T(8,128)(2,1)} %param.7) | copy-start | bytes 12582916
  144.4 2.2 %copy-start.5 = (bf16[1,64,16,2048]{3,2,1,0:T(8,128)(2,1)S(1)}, bf16[1,64,16,2048]{3,2,1,0:T(8,128)(2,1)}, u32[]{:S(2)}) copy-start(bf16[1,64,16,2048]{3,2,1,0:T(8,128)(2,1)} %param.8) | copy-start | bytes 12582916
  146.6 2.2 %copy-start.9 = (bf16[1024,2048]{1,0:T(8,128)(2,1)S(1)}, bf16[1024,2048]{1,0:T(8,128)(2,1)}, u32[]{:S(2)}) copy-start(bf16[1024,2048]{1,0:T(8,128)(2,1)} %copy-done.8) | copy-start | bytes 12582916
  148.8 4.0 %copy-start.3 = (bf16[1,64,16,2048]{3,2,1,0:T(8,128)(2,1)S(1)}, bf16[1,64,16,2048]{3,2,1,0:T(8,128)(2,1)}, u32[]{:S(2)}) copy-start(bf16[1,64,16,2048]{3,2,1,0:T(8,128)(2,1)} %param.7) | copy-start | bytes 12582916
  148.8 4.0 %copy-start.6 = (bf16[1,64,16,2048]{3,2,1,0:T(8,128)(2,1)S(1)}, bf16[1,64,16,2048]{3,2,1,0:T(8,128)(2,1)}, u32[]{:S(2)}) copy-start(bf16[1,64,16,2048]{3,2,1,0:T(8,128)(2,1)} %param.8) | copy-start | bytes 12582916

commit v2 on v1

v2 whole, which is shorter than its diff:
```python
import functools

import jax
import jax.numpy as jnp
from jax import lax
from jax.experimental import pallas as pl
from jax.experimental.pallas import tpu as pltpu
from jax.sharding import PartitionSpec as P

CHUNKS = ((512, 128), (256, 128))
BLOCK = 512
VMEM_LIMIT = 20 * 1024 * 1024


def mirror_pair(x):
    return lax.ppermute(x, "pair", [(i, i ^ 1) for i in range(lax.axis_size("pair"))])


def whole(count):
    return [pl.BlockSpec(memory_space=pltpu.VMEM)] * count


def scalars():
    return [pl.BlockSpec(memory_space=pltpu.SMEM)]


def params():
    return pltpu.CompilerParams(vmem_limit_bytes=VMEM_LIMIT)


def pack_kernel(table_ref, tiles_ref, out_ref):
    for k in range(out_ref.shape[0]):
        out_ref[k] = tiles_ref[table_ref[k]]


def pack(table, tiles):
    count = table.shape[0]
    return pl.pallas_call(
        pack_kernel,
        out_shape=jax.ShapeDtypeStruct((count,) + tiles.shape[1:], tiles.dtype),
        in_specs=scalars() + whole(1),
        out_specs=whole(1)[0],
        compiler_params=params(),
    )(table, tiles)


def window_kernel(begin, where_ref, received_ref, out_ref):
    width = out_ref.shape[2]
    for w in range(out_ref.shape[0]):
        place = where_ref[w]
        tile = received_ref[jnp.maximum(place, 0), :, begin : begin + width]
        out_ref[w] = jnp.where(place >= 0, tile, jnp.zeros_like(tile))


def unpack(where, received, begin, width):
    shape = where.shape + (received.shape[1], width)
    return pl.pallas_call(
        functools.partial(window_kernel, begin),
        out_shape=jax.ShapeDtypeStruct(shape, received.dtype),
        in_specs=scalars() + whole(1),
        out_specs=whole(1)[0],
        compiler_params=params(),
    )(where, received)


def turned_sums(own_ref, mirror_ref):
    slots, tile_width, width = own_ref.shape
    own = own_ref[...].reshape(slots * tile_width, width).astype(jnp.float32)
    mirrored = mirror_ref[...].reshape(slots * tile_width, width).astype(jnp.float32)
    plus = (own + mirrored).astype(jnp.bfloat16).T
    minus = (own - mirrored).astype(jnp.bfloat16).T
    return plus, minus


def product(plus, minus, plus_ref, minus_ref, across):
    depth = plus.shape[1]
    block = across.stop - across.start
    total = jnp.dot(
        plus, plus_ref[:, :, across].reshape(depth, block), preferred_element_type=jnp.float32
    )
    total = total + jnp.dot(
        minus, minus_ref[:, :, across].reshape(depth, block), preferred_element_type=jnp.float32
    )
    return (0.5 * total).astype(jnp.bfloat16)


def rows_kernel(own_ref, mirror_ref, plus_ref, minus_ref, out_ref):
    plus, minus = turned_sums(own_ref, mirror_ref)
    for begin in range(0, out_ref.shape[1], BLOCK):
        across = slice(begin, begin + BLOCK)
        out_ref[:, across] = product(plus, minus, plus_ref, minus_ref, across)


def cost(own, columns, more=0):
    depth = own.shape[0] * own.shape[1]
    return pl.CostEstimate(
        flops=4 * depth * own.shape[2] * columns + more,
        bytes_accessed=8 * depth * columns,
        transcendentals=0,
    )


def make_rows(own, mirrored, plus_slab, minus_slab):
    columns = plus_slab.shape[2]
    return pl.pallas_call(
        rows_kernel,
        out_shape=jax.ShapeDtypeStruct((own.shape[2], columns), jnp.bfloat16),
        in_specs=whole(4),
        out_specs=whole(1)[0],
        compiler_params=params(),
        cost_estimate=cost(own, columns),
    )(own, mirrored, plus_slab, minus_slab)


def finish_kernel(earlier, based, *refs):
    own_ref, mirror_ref, restore_ref, plus_ref, minus_ref = refs[:5]
    earlier_refs = refs[5 : 5 + earlier]
    refs = refs[5 + earlier :]
    if based:
        base_hbm, out_hbm, held, held_sems, based_on, base_sems = refs
    else:
        out_hbm, held, held_sems = refs
    blocks = range(held.shape[0])
    spans = [slice(b * BLOCK, b * BLOCK + BLOCK) for b in blocks]
    if based:
        loads = [
            pltpu.make_async_copy(base_hbm.at[:, spans[b]], based_on.at[b], base_sems.at[b])
            for b in blocks
        ]
        for load in loads:
            load.start()
    plus, minus = turned_sums(own_ref, mirror_ref)
    stores = []
    for b in blocks:
        parts = [ref[:, spans[b]] for ref in earlier_refs]
        parts.append(product(plus, minus, plus_ref, minus_ref, spans[b]))
        rows = parts[0] if len(parts) == 1 else jnp.concatenate(parts, axis=0)
        ladder = jnp.dot(restore_ref[...], rows, preferred_element_type=jnp.float32)
        if based:
            loads[b].wait()
            ladder = ladder + based_on[b].astype(jnp.float32)
        held[b] = ladder.astype(held.dtype)
        store = pltpu.make_async_copy(held.at[b], out_hbm.at[:, spans[b]], held_sems.at[b])
        store.start()
        stores.append(store)
    for store in stores:
        store.wait()


def finish(own, mirrored, restore, plus_slab, minus_slab, earlier, base):
    columns = plus_slab.shape[2]
    rows = restore.shape[0]
    blocks = columns // BLOCK
    in_hbm = pl.BlockSpec(memory_space=pltpu.HBM)
    held = [pltpu.VMEM((blocks, rows, BLOCK), jnp.bfloat16), pltpu.SemaphoreType.DMA((blocks,))]
    based = base is not None
    return pl.pallas_call(
        functools.partial(finish_kernel, len(earlier), based),
        out_shape=jax.ShapeDtypeStruct((rows, columns), jnp.bfloat16),
        in_specs=whole(5 + len(earlier)) + ([in_hbm] if based else []),
        out_specs=in_hbm,
        scratch_shapes=held * (2 if based else 1),
        compiler_params=params(),
        cost_estimate=cost(own, columns, 2 * rows * restore.shape[1] * columns),
    )(own, mirrored, restore, plus_slab, minus_slab, *earlier, *([base] if based else []))


def pin_kernel(slab_ref, out_ref, sem):
    copy = pltpu.make_async_copy(slab_ref, out_ref, sem)
    copy.start()
    copy.wait()


def pin(slab):
    return pl.pallas_call(
        pin_kernel,
        out_shape=pltpu.VMEM(slab.shape, slab.dtype),
        in_specs=[pl.BlockSpec(memory_space=pltpu.HBM)],
        out_specs=pl.BlockSpec(memory_space=pltpu.VMEM),
        scratch_shapes=[pltpu.SemaphoreType.DMA],
        compiler_params=params(),
    )(slab)


def route_plan(win_tile, win_count, me):
    slots = win_tile.shape[1]
    position = jnp.arange(slots)
    sources = win_tile >> 5
    mine = (sources == me) & (position[None, :] < win_count[:, None])
    coded = position[None, :] * 32 + (win_tile & 31)
    first = jnp.min(jnp.where(mine, coded, 1 << 20), axis=1) & 31
    last = jnp.maximum(jnp.max(jnp.where(mine, coded, -1), axis=1), 0) & 31
    send = jnp.stack([first, last], axis=1).reshape(-1)
    own = lax.dynamic_index_in_dim(sources, me, 0, keepdims=False)
    living = position < lax.dynamic_index_in_dim(win_count, me, 0, keepdims=False)
    earlier = (
        (own[:, None] == own[None, :])
        & living[None, :]
        & (position[None, :] < position[:, None])
    )
    rank = jnp.any(earlier, axis=1).astype(jnp.int32)
    return send, jnp.where(living, own * 2 + rank, -1)


def after(value, *others):
    return lax.optimization_barrier((value,) + others)[0]


def body(t2, v_plus, v_minus, partner, win_tile, win_count):
    tiles, tile_width, rows = t2.shape
    me = lax.axis_index("tiles")
    odd = lax.axis_index("pair") % 2 == 1
    index = jnp.arange(rows)
    order = jnp.where(odd, partner, index)
    send, where = route_plan(win_tile, win_count, me)
    flat = t2.reshape(tiles * tile_width, rows)
    begin = 0
    chunks, restores = [], []
    for pieces in CHUNKS:
        width = sum(pieces)
        select = (order[:, None] == index[None, begin : begin + width]).astype(jnp.bfloat16)
        chunk = jnp.dot(flat, select, preferred_element_type=jnp.float32).astype(jnp.bfloat16)
        chunks.append(chunk.reshape(tiles, tile_width, width))
        restores.append(select)
        begin += width
    landed = [lax.all_to_all(pack(send, chunks[0]), "tiles", 0, 0, tiled=True)]
    early = tuple(restores) + (where,) + tuple(chunks[1:])
    plus_slab = pin(after(v_plus[0], *early))
    minus_slab = pin(after(v_minus[0], *early))
    for chunk in chunks[1:]:
        outgoing = pack(send, after(chunk, plus_slab, minus_slab))
        outgoing = after(outgoing, landed[-1])
        landed.append(lax.all_to_all(outgoing, "tiles", 0, 0, tiled=True))
    ladder = None
    earlier = []
    for pieces, received, restore in zip(CHUNKS, landed, restores, strict=True):
        if earlier:
            received = after(received, earlier[-1])
        inner = 0
        pairs = []
        for width in pieces:
            own = unpack(where, received, inner, width)
            pairs.append((own, mirror_pair(own)))
            inner += width
        earlier = [make_rows(*pair, plus_slab, minus_slab) for pair in pairs[:-1]]
        ladder = finish(*pairs[-1], restore, plus_slab, minus_slab, earlier, ladder)
    return ladder


def solution(mesh):
    placed = (
        P("tiles", None, "pair"),
        P("tiles", None, None, None),
        P("tiles", None, None, None),
        P("pair"),
        P(),
        P(),
    )
    return jax.shard_map(
        body, mesh=mesh, in_specs=placed, out_specs=P("pair", "tiles"), check_vma=False
    )
```

time: 159 us -> 152 us (0.956)
  waiting for transfers between devices: 81.1 us -> 74.7 us
  starting transfers between devices: 26 us -> 22.2 us
  local copies, waits for them, and re-layouts: 15.6 us -> 19.2 us
    all_to_all x3 -> x2, waiting for transfers between devices: 81 us -> 51.5 us  [the longest x1 47.7 us: body(): landed = [lax.all_to_all(pack(send, chunks[0]), 'tiles', 0, 0, tiled=True)]]
    ppermute x3 -> x4, waiting for transfers between devices: 0.12 us -> 23.2 us  [mirror_pair(): lax.ppermute(x, 'pair', [(i, i ^ 1) for i in range(lax.axis_size('pair'))])]
    all_to_all x3 -> x2, starting transfers between devices: 23.4 us -> 17.7 us  [the longest x1 12.3 us: body(): landed = [lax.all_to_all(pack(send, chunks[0]), 'tiles', 0, 0, tiled=True)]]
    unnamed x22 -> x32, local copies, waits for them, and re-layouts: 14.5 us -> 18.1 us
    pallas_call x3 -> x2, Pallas kernels: 3.84 us -> 1.48 us  [pack(): pl.pallas_call(pack_kernel, out_shape=jax.ShapeDtypeStruct((count,) + til...]
    ppermute x3 -> x4, starting transfers between devices: 2.57 us -> 4.49 us  [mirror_pair(): lax.ppermute(x, 'pair', [(i, i ^ 1) for i in range(lax.axis_size('pair'))])]
    pallas_call x6 -> x10, Pallas kernels: 24.5 us -> 26.3 us  [the longest x2 12.7 us: finish(): pl.pallas_call(functools.partial(finish_kernel, len(earlier), based), out...]
  transfers between devices with their start and end apart: 6 -> 6, of which waited for: 3 -> 5; matrix products, arithmetic and copies ran while one was open for 3% -> 3% of each run, Pallas kernels for 14% -> 14%
where the time goes in v2:
time: 152 us; the launch traced here: 151 us
  waiting for transfers between devices  74.7 us (49%)
  Pallas kernels  27.7 us (18%)
  starting transfers between devices  22.2 us (15%)
  local copies, waits for them, and re-layouts  19.2 us (13%)
  other arithmetic  4.8 us (3%)
  matrix products  1.95 us (1%)
    all_to_all x1, waiting for transfers between devices, body(): landed = [lax.all_to_all(pack(send, chunks[0]), 'tiles', 0, 0, tiled=True)]  47.7 us
    ppermute x4, waiting for transfers between devices, mirror_pair(): lax.ppermute(x, 'pair', [(i, i ^ 1) for i in range(lax.axis_size('pair'))])  23.2 us
    unnamed x32, local copies, waits for them, and re-layouts  18.1 us
    pallas_call x2, Pallas kernels, finish(): pl.pallas_call(functools.partial(finish_kernel, len(earlier), based), out...  12.7 us
    all_to_all x1, starting transfers between devices, body(): landed = [lax.all_to_all(pack(send, chunks[0]), 'tiles', 0, 0, tiled=True)]  12.3 us
    pallas_call x2, Pallas kernels, make_rows(): pl.pallas_call(rows_kernel, out_shape=jax.ShapeDtypeStruct((own.shape[2],...  6.91 us
    pallas_call x4, Pallas kernels, unpack(): pl.pallas_call(functools.partial(window_kernel, begin), out_shape=jax.Sha...  6.04 us
    all_to_all x1, starting transfers between devices, body(): landed.append(lax.all_to_all(outgoing, 'tiles', 0, 0, tiled=True))  5.42 us
  transfers between devices with their start and end apart: 6, of which 5 were waited for; matrix products, arithmetic and copies ran while one was open for 3% of the time, Pallas kernels for 14%

profile of v2, /device:TPU:28, one launch (start us, length us, event | category | flops | bytes accessed | tf_op | source)
XLA Modules:
  0.0 151.0 jit_solution(3528041749580399744)
XLA Ops:
  0.0 1.0 select_reduce_fusion.1
  1.3 0.7 iota_select_fusion
  2.0 1.1 fusion.2
  3.1 0.8 shard_map.67
  3.9 1.5 %copy-done.8 = bf16[128,16,640]{2,1,0:T(8,128)(2,1)} copy-done((bf16[128,16,640]{2,1,0:T(8,128)(2,1)}, bf16[128,16,640]{2,1,0:T(8,128)(2,1)S(1)}, u32[]{:S(2)}) %copy-start.8) | copy-done | bytes 2621464
  5.4 12.3 %all-to-all-start = ((bf16[128,16,640]{2,1,0:T(8,128)(2,1)}), bf16[128,16,640]{2,1,0:T(8,128)(2,1)}, u32[]{:S(2)}, u32[]{:S(2)}) async-start(bf16[128,16,640]{2,1,0:T(8,128)(2,1)} %copy-done.8), calls=%async_computation | async-start | bytes 5242880 | tf_op jit(solution)/shard_map/all_to_all | solution.py:226
  18.4 0.8 fusion.7
  21.2 1.4 compare_convert_fusion.refs_2_
  22.5 2.2 %copy-done.11 = bf16[1,64,16,2048]{3,2,1,0:T(8,128)(2,1)S(1)} copy-done((bf16[1,64,16,2048]{3,2,1,0:T(8,128)(2,1)S(1)}, bf16[1,64,16,2048]{3,2,1,0:T(8,128)(2,1)}, u32[]{:S(2)}) %copy-start.11) | copy-done | bytes 4194328
  25.0 2.1 %copy-done.1 = bf16[64,16,2048]{2,1,0:T(8,128)(2,1)} copy-done((bf16[64,16,2048]{2,1,0:T(8,128)(2,1)}, bf16[64,16,2048]{2,1,0:T(8,128)(2,1)S(1)}, u32[]{:S(2)}) %copy-start.1) | copy-done | bytes 4194328
  27.1 1.3 copy-done.12
  28.7 2.0 %copy-done.5 = bf16[64,16,2048]{2,1,0:T(8,128)(2,1)} copy-done((bf16[64,16,2048]{2,1,0:T(8,128)(2,1)}, bf16[64,16,2048]{2,1,0:T(8,128)(2,1)S(1)}, u32[]{:S(2)}) %copy-start.5) | copy-done | bytes 4194328
  30.7 0.7 shard_map.66
  31.4 1.1 copy-done.9
  32.5 47.7 %all-to-all-done.received_ref = bf16[128,16,640]{2,1,0:T(8,128)(2,1)} async-done(((bf16[128,16,640]{2,1,0:T(8,128)(2,1)}), bf16[128,16,640]{2,1,0:T(8,128)(2,1)}, u32[]{:S(2)}, u32[]{:S(2)}) %all-to-all-start) | async-done | bytes 2621472 | tf_op jit(solution)/shard_map/all_to_all | solution.py:226
  80.2 5.4 %all-to-all-start.1 = ((bf16[128,16,384]{2,1,0:T(8,128)(2,1)}), bf16[128,16,384]{2,1,0:T(8,128)(2,1)S(1)}, u32[]{:S(2)}, u32[]{:S(2)}) async-start(bf16[128,16,384]{2,1,0:T(8,128)(2,1)} %copy-done.9), calls=%async_computation.1 | async-start | bytes 3145728 | tf_op jit(solution)/shard_map/all_to_all | solution.py:233
  85.6 2.0 %shard_map.68.own_ref = bf16[64,16,512]{2,1,0:T(8,128)(2,1)S(1)} custom-call(s32[64]{0:T(128)S(1)} %add_select_fusion.where_ref, bf16[128,16,640]{2,1,0:T(8,128)(2,1)} %all-to-all-done.received_ref), custom_call_target="tpu_custom_call" | custom-call | tf_op jit(solution)/shard_map/pallas_call | solution.py:57
  87.9 2.6 %shard_map.73.refs_0_ = bf16[64,16,128]{2,1,0:T(8,128)(2,1)} custom-call(s32[64]{0:T(128)S(1)} %add_select_fusion.where_ref, bf16[128,16,640]{2,1,0:T(8,128)(2,1)} %all-to-all-done.received_ref), custom_call_target="tpu_custom_call" | custom-call | tf_op jit(solution)/shard_map/pallas_call | solution.py:57
  90.5 1.9 %collective-permute-start.3 = (bf16[64,16,128]{2,1,0:T(8,128)(2,1)}, bf16[64,16,128]{2,1,0:T(8,128)(2,1)}, u32[]{:S(2)}, u32[]{:S(2)}) collective-permute-start(bf16[64,16,128]{2,1,0:T(8,128)(2,1)} %shard_map.73.refs_0_), channel_id=1, source_target_pairs={{0,1},{1,0},{2,3},{3,2},{4,5},{5,4},{6,7},{7,6},{8,9},{9,8},{10,11... | collective-permute-start | bytes 786440 | tf_op jit(solution)/shard_map/ppermute | solution.py:16
  92.4 21.4 %collective-permute-done.mirror_ref = bf16[64,16,512]{2,1,0:T(8,128)(2,1)S(1)} collective-permute-done((bf16[64,16,512]{2,1,0:T(8,128)(2,1)S(1)}, bf16[64,16,512]{2,1,0:T(8,128)(2,1)S(1)}, u32[]{:S(2)}, u32[]{:S(2)}) %collective-permute-start) | collective-permute-done | bytes 1048608 | tf_op jit(solution)/shard_map/ppermute | solution.py:16
  113.8 2.2 %copy-done.6 = bf16[64,16,2048]{2,1,0:T(8,128)(2,1)S(1)} copy-done((bf16[64,16,2048]{2,1,0:T(8,128)(2,1)S(1)}, bf16[64,16,2048]{2,1,0:T(8,128)(2,1)}, u32[]{:S(2)}) %copy-start.6) | copy-done | bytes 4194328
  116.0 4.5 %shard_map.69.refs_5_ = bf16[512,2048]{1,0:T(8,128)(2,1)S(1)} custom-call(bf16[64,16,512]{2,1,0:T(8,128)(2,1)S(1)} %shard_map.68.own_ref, bf16[64,16,512]{2,1,0:T(8,128)(2,1)S(1)} %collective-permute-done.mirror_ref, bf16[64,16,2048]{2,1,0:T(8,128)(2,1)S(1)} %copy-done.2, bf16[64,16,2048]{2,1,0:T(8,128)(2,1)S(1)} %copy-done.6), custom_call_target="tpu_custom_call" | custom-call | flops 4294967296 | bytes 16777216 | tf_op jit(solution)/shard_map/pallas_call | solution.py:105
  120.5 1.3 copy-done.13
  121.9 3.8 %all-to-all-done.1.received_ref = bf16[128,16,384]{2,1,0:T(8,128)(2,1)S(1)} async-done(((bf16[128,16,384]{2,1,0:T(8,128)(2,1)}), bf16[128,16,384]{2,1,0:T(8,128)(2,1)S(1)}, u32[]{:S(2)}, u32[]{:S(2)}) %all-to-all-start.1) | async-done | bytes 1572896 | tf_op jit(solution)/shard_map/all_to_all | solution.py:233
  126.5 0.7 shard_map.70.refs_0_
  127.2 2.2 %collective-permute-start.1 = (bf16[64,16,128]{2,1,0:T(8,128)(2,1)S(1)}, bf16[64,16,128]{2,1,0:T(8,128)(2,1)S(1)}, u32[]{:S(2)}, u32[]{:S(2)}) collective-permute-start(bf16[64,16,128]{2,1,0:T(8,128)(2,1)S(1)} %shard_map.70.refs_0_), channel_id=1, source_target_pairs={{0,1},{1,0},{2,3},{3,2},{4,5},{5,4},{6,7},{7,6},{8,9},{9,8},{10,11... | collective-permute-start | bytes 786440 | tf_op jit(solution)/shard_map/ppermute | solution.py:16
  129.5 2.2 %copy-done.3 = bf16[64,16,2048]{2,1,0:T(8,128)(2,1)S(1)} copy-done((bf16[64,16,2048]{2,1,0:T(8,128)(2,1)S(1)}, bf16[64,16,2048]{2,1,0:T(8,128)(2,1)}, u32[]{:S(2)}) %copy-start.3) | copy-done | bytes 4194328
  131.6 2.2 %copy-done.7 = bf16[64,16,2048]{2,1,0:T(8,128)(2,1)S(1)} copy-done((bf16[64,16,2048]{2,1,0:T(8,128)(2,1)S(1)}, bf16[64,16,2048]{2,1,0:T(8,128)(2,1)}, u32[]{:S(2)}) %copy-start.7) | copy-done | bytes 4194328
  133.8 6.8 %shard_map.74.refs_6_ = bf16[1024,2048]{1,0:T(8,128)(2,1)S(1)} custom-call(bf16[64,16,128]{2,1,0:T(8,128)(2,1)} %shard_map.73.refs_0_, bf16[64,16,128]{2,1,0:T(8,128)(2,1)} %collective-permute-done.3.refs_1_, bf16[1024,640]{1,0:T(8,128)(2,1)S(1)} %copy-done.10, bf16[64,16,2048]{2,1,0:T(8,128)(2,1)S(1)} %copy-done.3, bf16[64,16,2048]{2,1,0:T(8,128)(2,1)S(1)} %copy-done.7, ...), custom_call_target="tpu_custom_call" | custom-call | flops 3758096384 | bytes 16777216 | tf_op jit(solution)/shard_map/pallas_call | solution.py:157
  141.3 2.4 %shard_map.72.refs_5_ = bf16[256,2048]{1,0:T(8,128)(2,1)S(1)} custom-call(bf16[64,16,256]{2,1,0:T(8,128)(2,1)S(1)} %shard_map.71.own_ref, bf16[64,16,256]{2,1,0:T(8,128)(2,1)S(1)} %collective-permute-done.2.mirror_ref, bf16[64,16,2048]{2,1,0:T(8,128)(2,1)S(1)} %copy-done.3, bf16[64,16,2048]{2,1,0:T(8,128)(2,1)S(1)} %copy-done.7), custom_call_target="tpu_custom_call" | custom-call | flops 2147483648 | bytes 16777216 | tf_op jit(solution)/shard_map/pallas_call | solution.py:105
  143.7 1.2 collective-permute-done.1.refs_1_
  144.9 5.9 %shard_map.75 = bf16[1024,2048]{1,0:T(8,128)(2,1)} custom-call(bf16[64,16,128]{2,1,0:T(8,128)(2,1)S(1)} %shard_map.70.refs_0_, bf16[64,16,128]{2,1,0:T(8,128)(2,1)S(1)} %collective-permute-done.1.refs_1_, bf16[1024,384]{1,0:T(8,128)(2,1)S(1)} %compare_convert_fusion.1.refs_2_, bf16[64,16,2048]{2,1,0:T(8,128)(2,1)S(1)} %copy-done.4, ...), custom_call_target="tpu_custom_call" | custom-call | flops 2684354560 | bytes 16777216 | tf_op jit(solution)/shard_map/pallas_call | solution.py:157
  (44 shorter events, 5.1 us)
Async XLA Ops:
  0.0 2.0 %copy-start = (bf16[32,16,1024]{2,1,0:T(8,128)(2,1)S(1)}, bf16[32,16,1024]{2,1,0:T(8,128)(2,1)}, u32[]{:S(2)}) copy-start(bf16[32,16,1024]{2,1,0:T(8,128)(2,1)} %param.6) | copy-start | bytes 3145732
  3.9 1.5 %copy-start.8 = (bf16[128,16,640]{2,1,0:T(8,128)(2,1)}, bf16[128,16,640]{2,1,0:T(8,128)(2,1)S(1)}, u32[]{:S(2)}) copy-start(bf16[128,16,640]{2,1,0:T(8,128)(2,1)S(1)} %shard_map.67) | copy-start | bytes 7864324
  5.4 12.3 %copy-start.15 = (s32[64]{0:T(128)S(1)}, s32[64]{0:T(128)}, u32[]{:S(2)}) copy-start(s32[64]{0:T(128)} %param.11) | copy-start | bytes 772
  5.4 74.7 %all-to-all-start = ((bf16[128,16,640]{2,1,0:T(8,128)(2,1)}), bf16[128,16,640]{2,1,0:T(8,128)(2,1)}, u32[]{:S(2)}, u32[]{:S(2)}) async-start(bf16[128,16,640]{2,1,0:T(8,128)(2,1)} %copy-done.8), calls=%async_computation | async-start | bytes 5242880 | tf_op jit(solution)/shard_map/all_to_all | solution.py:226
  22.5 2.2 %copy-start.11 = (bf16[1,64,16,2048]{3,2,1,0:T(8,128)(2,1)S(1)}, bf16[1,64,16,2048]{3,2,1,0:T(8,128)(2,1)}, u32[]{:S(2)}) copy-start(bf16[1,64,16,2048]{3,2,1,0:T(8,128)(2,1)} %param.7) | copy-start | bytes 12582916
  24.7 3.7 %copy-start.12 = (bf16[1,64,16,2048]{3,2,1,0:T(8,128)(2,1)S(1)}, bf16[1,64,16,2048]{3,2,1,0:T(8,128)(2,1)}, u32[]{:S(2)}) copy-start(bf16[1,64,16,2048]{3,2,1,0:T(8,128)(2,1)} %param.8) | copy-start | bytes 12582916
  25.0 2.1 %copy-start.1 = (bf16[64,16,2048]{2,1,0:T(8,128)(2,1)}, bf16[64,16,2048]{2,1,0:T(8,128)(2,1)S(1)}, u32[]{:S(2)}) copy-start(bf16[64,16,2048]{2,1,0:T(8,128)(2,1)S(1)} %shard_map.64.plus_ref.refs_3_) | copy-start | bytes 12582916
  28.7 2.0 %copy-start.5 = (bf16[64,16,2048]{2,1,0:T(8,128)(2,1)}, bf16[64,16,2048]{2,1,0:T(8,128)(2,1)S(1)}, u32[]{:S(2)}) copy-start(bf16[64,16,2048]{2,1,0:T(8,128)(2,1)S(1)} %shard_map.65.minus_ref.refs_4_) | copy-start | bytes 12582916
  31.4 1.1 copy-start.9
  80.2 45.5 %all-to-all-start.1 = ((bf16[128,16,384]{2,1,0:T(8,128)(2,1)}), bf16[128,16,384]{2,1,0:T(8,128)(2,1)S(1)}, u32[]{:S(2)}, u32[]{:S(2)}) async-start(bf16[128,16,384]{2,1,0:T(8,128)(2,1)} %copy-done.9), calls=%async_computation.1 | async-start | bytes 3145728 | tf_op jit(solution)/shard_map/all_to_all | solution.py:233
  85.6 28.2 %copy-start.2 = (bf16[64,16,2048]{2,1,0:T(8,128)(2,1)S(1)}, bf16[64,16,2048]{2,1,0:T(8,128)(2,1)}, u32[]{:S(2)}) copy-start(bf16[64,16,2048]{2,1,0:T(8,128)(2,1)} %copy-done.1) | copy-start | bytes 12582916
  87.7 26.1 %collective-permute-start = (bf16[64,16,512]{2,1,0:T(8,128)(2,1)S(1)}, bf16[64,16,512]{2,1,0:T(8,128)(2,1)S(1)}, u32[]{:S(2)}, u32[]{:S(2)}) collective-permute-start(bf16[64,16,512]{2,1,0:T(8,128)(2,1)S(1)} %shard_map.68.own_ref), channel_id=1, source_target_pairs={{0,1},{1,0},{2,3},{3,2},{4,5},{5,4},{6,7},{7,6},{8,9},{9,8},{10,11... | collective-permute-start | bytes 3145736 | tf_op jit(solution)/shard_map/ppermute | solution.py:16
  90.5 39.0 %collective-permute-start.3 = (bf16[64,16,128]{2,1,0:T(8,128)(2,1)}, bf16[64,16,128]{2,1,0:T(8,128)(2,1)}, u32[]{:S(2)}, u32[]{:S(2)}) collective-permute-start(bf16[64,16,128]{2,1,0:T(8,128)(2,1)} %shard_map.73.refs_0_), channel_id=1, source_target_pairs={{0,1},{1,0},{2,3},{3,2},{4,5},{5,4},{6,7},{7,6},{8,9},{9,8},{10,11... | collective-permute-start | bytes 786440 | tf_op jit(solution)/shard_map/ppermute | solution.py:16
  113.8 2.2 %copy-start.6 = (bf16[64,16,2048]{2,1,0:T(8,128)(2,1)S(1)}, bf16[64,16,2048]{2,1,0:T(8,128)(2,1)}, u32[]{:S(2)}) copy-start(bf16[64,16,2048]{2,1,0:T(8,128)(2,1)} %copy-done.5) | copy-start | bytes 12582916
  120.5 1.4 copy-start.13
  125.7 3.8 %copy-start.10 = (bf16[1024,640]{1,0:T(8,128)(2,1)S(1)}, bf16[1024,640]{1,0:T(8,128)(2,1)}, u32[]{:S(2)}) copy-start(bf16[1024,640]{1,0:T(8,128)(2,1)} %compare_convert_fusion.refs_2_) | copy-start | bytes 3932164
  125.7 3.8 %copy-start.14 = (bf16[512,2048]{1,0:T(8,128)(2,1)S(1)}, bf16[512,2048]{1,0:T(8,128)(2,1)}, u32[]{:S(2)}) copy-start(bf16[512,2048]{1,0:T(8,128)(2,1)} %copy-done.13) | copy-start | bytes 6291460
  126.4 14.9 %collective-permute-start.2 = (bf16[64,16,256]{2,1,0:T(8,128)(2,1)S(1)}, bf16[64,16,256]{2,1,0:T(8,128)(2,1)S(1)}, u32[]{:S(2)}, u32[]{:S(2)}) collective-permute-start(bf16[64,16,256]{2,1,0:T(8,128)(2,1)S(1)} %shard_map.71.own_ref), channel_id=1, source_target_pairs={{0,1},{1,0},{2,3},{3,2},{4,5},{5,4},{6,7},{7,6},{8,9},{9,8},{10,11... | collective-permute-start | bytes 1572872 | tf_op jit(solution)/shard_map/ppermute | solution.py:16
  127.2 17.7 %collective-permute-start.1 = (bf16[64,16,128]{2,1,0:T(8,128)(2,1)S(1)}, bf16[64,16,128]{2,1,0:T(8,128)(2,1)S(1)}, u32[]{:S(2)}, u32[]{:S(2)}) collective-permute-start(bf16[64,16,128]{2,1,0:T(8,128)(2,1)S(1)} %shard_map.70.refs_0_), channel_id=1, source_target_pairs={{0,1},{1,0},{2,3},{3,2},{4,5},{5,4},{6,7},{7,6},{8,9},{9,8},{10,11... | collective-permute-start | bytes 786440 | tf_op jit(solution)/shard_map/ppermute | solution.py:16
  129.4 2.2 %copy-start.3 = (bf16[64,16,2048]{2,1,0:T(8,128)(2,1)S(1)}, bf16[64,16,2048]{2,1,0:T(8,128)(2,1)}, u32[]{:S(2)}) copy-start(bf16[64,16,2048]{2,1,0:T(8,128)(2,1)} %copy-done.1) | copy-start | bytes 12582916
  131.6 2.2 %copy-start.7 = (bf16[64,16,2048]{2,1,0:T(8,128)(2,1)S(1)}, bf16[64,16,2048]{2,1,0:T(8,128)(2,1)}, u32[]{:S(2)}) copy-start(bf16[64,16,2048]{2,1,0:T(8,128)(2,1)} %copy-done.5) | copy-start | bytes 12582916
  141.3 3.6 %copy-start.4 = (bf16[64,16,2048]{2,1,0:T(8,128)(2,1)S(1)}, bf16[64,16,2048]{2,1,0:T(8,128)(2,1)}, u32[]{:S(2)}) copy-start(bf16[64,16,2048]{2,1,0:T(8,128)(2,1)} %copy-done.1) | copy-start | bytes 12582916

commit v3 on v2

--- a/solution.py
+++ b/solution.py
@@ -112,57 +112,50 @@
     )(own, mirrored, plus_slab, minus_slab)
 
 
-def finish_kernel(earlier, based, *refs):
+def finish_kernel(earlier, based, last, *refs):
     own_ref, mirror_ref, restore_ref, plus_ref, minus_ref = refs[:5]
     earlier_refs = refs[5 : 5 + earlier]
-    refs = refs[5 + earlier :]
-    if based:
-        base_hbm, out_hbm, held, held_sems, based_on, base_sems = refs
-    else:
-        out_hbm, held, held_sems = refs
-    blocks = range(held.shape[0])
-    spans = [slice(b * BLOCK, b * BLOCK + BLOCK) for b in blocks]
-    if based:
-        loads = [
-            pltpu.make_async_copy(base_hbm.at[:, spans[b]], based_on.at[b], base_sems.at[b])
-            for b in blocks
-        ]
-        for load in loads:
-            load.start()
+    base_ref = refs[5 + earlier] if based else None
+    refs = refs[5 + earlier + based :]
     plus, minus = turned_sums(own_ref, mirror_ref)
     stores = []
-    for b in blocks:
-        parts = [ref[:, spans[b]] for ref in earlier_refs]
-        parts.append(product(plus, minus, plus_ref, minus_ref, spans[b]))
+    for b in range(plus_ref.shape[2] // BLOCK):
+        across = slice(b * BLOCK, b * BLOCK + BLOCK)
+        parts = [ref[:, across] for ref in earlier_refs]
+        parts.append(product(plus, minus, plus_ref, minus_ref, across))
         rows = parts[0] if len(parts) == 1 else jnp.concatenate(parts, axis=0)
         ladder = jnp.dot(restore_ref[...], rows, preferred_element_type=jnp.float32)
         if based:
-            loads[b].wait()
-            ladder = ladder + based_on[b].astype(jnp.float32)
-        held[b] = ladder.astype(held.dtype)
-        store = pltpu.make_async_copy(held.at[b], out_hbm.at[:, spans[b]], held_sems.at[b])
-        store.start()
-        stores.append(store)
+            ladder = ladder + base_ref[:, across].astype(jnp.float32)
+        if last:
+            out_hbm, held, sems = refs
+            held[b] = ladder.astype(held.dtype)
+            store = pltpu.make_async_copy(held.at[b], out_hbm.at[:, across], sems.at[b])
+            store.start()
+            stores.append(store)
+        else:
+            refs[0][:, across] = ladder.astype(jnp.bfloat16)
     for store in stores:
         store.wait()
 
 
-def finish(own, mirrored, restore, plus_slab, minus_slab, earlier, base):
+def finish(own, mirrored, restore, plus_slab, minus_slab, earlier, base, last):
     columns = plus_slab.shape[2]
     rows = restore.shape[0]
     blocks = columns // BLOCK
-    in_hbm = pl.BlockSpec(memory_space=pltpu.HBM)
+    operands = [own, mirrored, restore, plus_slab, minus_slab, *earlier]
+    if base is not None:
+        operands.append(base)
     held = [pltpu.VMEM((blocks, rows, BLOCK), jnp.bfloat16), pltpu.SemaphoreType.DMA((blocks,))]
-    based = base is not None
-    return pl.pallas_call(
-        functools.partial(finish_kernel, len(earlier), based),
+    return pl.pallas_call(
+        functools.partial(finish_kernel, len(earlier), base is not None, last),
         out_shape=jax.ShapeDtypeStruct((rows, columns), jnp.bfloat16),
-        in_specs=whole(5 + len(earlier)) + ([in_hbm] if based else []),
-        out_specs=in_hbm,
-        scratch_shapes=held * (2 if based else 1),
+        in_specs=whole(len(operands)),
+        out_specs=pl.BlockSpec(memory_space=pltpu.HBM if last else pltpu.VMEM),
+        scratch_shapes=held if last else [],
         compiler_params=params(),
         cost_estimate=cost(own, columns, 2 * rows * restore.shape[1] * columns),
-    )(own, mirrored, restore, plus_slab, minus_slab, *earlier, *([base] if based else []))
+    )(*operands)
 
 
 def pin_kernel(slab_ref, out_ref, sem):
@@ -232,10 +225,13 @@
         outgoing = after(outgoing, landed[-1])
         landed.append(lax.all_to_all(outgoing, "tiles", 0, 0, tiled=True))
     ladder = None
+    ladder = None
+    begin = 0
     earlier = []
     for pieces, received, restore in zip(CHUNKS, landed, restores, strict=True):
         if earlier:
             received = after(received, earlier[-1])
+        begin += restore.shape[1]
         inner = 0
         pairs = []
         for width in pieces:
@@ -243,7 +239,7 @@
             pairs.append((own, mirror_pair(own)))
             inner += width
         earlier = [make_rows(*pair, plus_slab, minus_slab) for pair in pairs[:-1]]
-        ladder = finish(*pairs[-1], restore, plus_slab, minus_slab, earlier, ladder)
+        ladder = finish(*pairs[-1], restore, plus_slab, minus_slab, earlier, ladder, begin == rows)
     return ladder
 
 

time: 152 us -> 150 us (0.987)
  Pallas kernels: 27.7 us -> 25 us
    pallas_call x2, Pallas kernels: 12.7 us -> 10 us  [finish(): pl.pallas_call(functools.partial(finish_kernel, len(earlier), base is not...]
  transfers between devices with their start and end apart: 6 -> 6, of which waited for: 5 -> 5; matrix products, arithmetic and copies ran while one was open for 3% -> 3% of each run, Pallas kernels for 14% -> 13%
where the time goes in v3:
time: 150 us
  waiting for transfers between devices  75.9 us (51%)
  Pallas kernels  25 us (17%)
  starting transfers between devices  22.2 us (15%)
  local copies, waits for them, and re-layouts  19.2 us (13%)
  other arithmetic  4.8 us (3%)
  matrix products  1.96 us (1%)
    all_to_all x1, waiting for transfers between devices, body(): landed = [lax.all_to_all(pack(send, chunks[0]), 'tiles', 0, 0, tiled=True)]  47.7 us
    ppermute x4, waiting for transfers between devices, mirror_pair(): lax.ppermute(x, 'pair', [(i, i ^ 1) for i in range(lax.axis_size('pair'))])  24.5 us
    unnamed x32, local copies, waits for them, and re-layouts  18.1 us
    all_to_all x1, starting transfers between devices, body(): landed = [lax.all_to_all(pack(send, chunks[0]), 'tiles', 0, 0, tiled=True)]  12.3 us
    pallas_call x2, Pallas kernels, finish(): pl.pallas_call(functools.partial(finish_kernel, len(earlier), base is not...  10 us
    pallas_call x2, Pallas kernels, make_rows(): pl.pallas_call(rows_kernel, out_shape=jax.ShapeDtypeStruct((own.shape[2],...  6.91 us
    pallas_call x4, Pallas kernels, unpack(): pl.pallas_call(functools.partial(window_kernel, begin), out_shape=jax.Sha...  6.04 us
    all_to_all x1, starting transfers between devices, body(): landed.append(lax.all_to_all(outgoing, 'tiles', 0, 0, tiled=True))  5.42 us
  transfers between devices with their start and end apart: 6, of which 5 were waited for; matrix products, arithmetic and copies ran while one was open for 3% of the time, Pallas kernels for 13%

profile of v3, /device:TPU:28, one launch (start us, length us, event | category | flops | bytes accessed | tf_op | source)
XLA Modules:
  0.0 149.5 jit_solution(15250314129577258056)
XLA Ops:
  0.0 1.0 select_reduce_fusion.1
  1.3 0.7 iota_select_fusion
  2.0 1.1 fusion.2
  3.1 0.8 shard_map.67
  3.9 1.5 %copy-done.8 = bf16[128,16,640]{2,1,0:T(8,128)(2,1)} copy-done((bf16[128,16,640]{2,1,0:T(8,128)(2,1)}, bf16[128,16,640]{2,1,0:T(8,128)(2,1)S(1)}, u32[]{:S(2)}) %copy-start.8) | copy-done | bytes 2621464
  5.4 12.3 %all-to-all-start = ((bf16[128,16,640]{2,1,0:T(8,128)(2,1)}), bf16[128,16,640]{2,1,0:T(8,128)(2,1)}, u32[]{:S(2)}, u32[]{:S(2)}) async-start(bf16[128,16,640]{2,1,0:T(8,128)(2,1)} %copy-done.8), calls=%async_computation | async-start | bytes 5242880 | tf_op jit(solution)/shard_map/all_to_all | solution.py:219
  18.4 0.8 fusion.7
  21.2 1.4 compare_convert_fusion.refs_2_
  22.5 2.2 %copy-done.11 = bf16[1,64,16,2048]{3,2,1,0:T(8,128)(2,1)S(1)} copy-done((bf16[1,64,16,2048]{3,2,1,0:T(8,128)(2,1)S(1)}, bf16[1,64,16,2048]{3,2,1,0:T(8,128)(2,1)}, u32[]{:S(2)}) %copy-start.11) | copy-done | bytes 4194328
  25.0 2.1 %copy-done.1 = bf16[64,16,2048]{2,1,0:T(8,128)(2,1)} copy-done((bf16[64,16,2048]{2,1,0:T(8,128)(2,1)}, bf16[64,16,2048]{2,1,0:T(8,128)(2,1)S(1)}, u32[]{:S(2)}) %copy-start.1) | copy-done | bytes 4194328
  27.1 1.3 copy-done.12
  28.7 2.0 %copy-done.5 = bf16[64,16,2048]{2,1,0:T(8,128)(2,1)} copy-done((bf16[64,16,2048]{2,1,0:T(8,128)(2,1)}, bf16[64,16,2048]{2,1,0:T(8,128)(2,1)S(1)}, u32[]{:S(2)}) %copy-start.5) | copy-done | bytes 4194328
  30.7 0.7 shard_map.66
  31.4 1.1 copy-done.9
  32.5 47.7 %all-to-all-done.received_ref = bf16[128,16,640]{2,1,0:T(8,128)(2,1)} async-done(((bf16[128,16,640]{2,1,0:T(8,128)(2,1)}), bf16[128,16,640]{2,1,0:T(8,128)(2,1)}, u32[]{:S(2)}, u32[]{:S(2)}) %all-to-all-start) | async-done | bytes 2621472 | tf_op jit(solution)/shard_map/all_to_all | solution.py:219
  80.2 5.4 %all-to-all-start.1 = ((bf16[128,16,384]{2,1,0:T(8,128)(2,1)}), bf16[128,16,384]{2,1,0:T(8,128)(2,1)S(1)}, u32[]{:S(2)}, u32[]{:S(2)}) async-start(bf16[128,16,384]{2,1,0:T(8,128)(2,1)} %copy-done.9), calls=%async_computation.1 | async-start | bytes 3145728 | tf_op jit(solution)/shard_map/all_to_all | solution.py:226
  85.6 2.0 %shard_map.68.own_ref = bf16[64,16,512]{2,1,0:T(8,128)(2,1)S(1)} custom-call(s32[64]{0:T(128)S(1)} %add_select_fusion.where_ref, bf16[128,16,640]{2,1,0:T(8,128)(2,1)} %all-to-all-done.received_ref), custom_call_target="tpu_custom_call" | custom-call | tf_op jit(solution)/shard_map/pallas_call | solution.py:57
  87.9 2.6 %shard_map.73.refs_0_ = bf16[64,16,128]{2,1,0:T(8,128)(2,1)} custom-call(s32[64]{0:T(128)S(1)} %add_select_fusion.where_ref, bf16[128,16,640]{2,1,0:T(8,128)(2,1)} %all-to-all-done.received_ref), custom_call_target="tpu_custom_call" | custom-call | tf_op jit(solution)/shard_map/pallas_call | solution.py:57
  90.5 1.9 %collective-permute-start.3 = (bf16[64,16,128]{2,1,0:T(8,128)(2,1)}, bf16[64,16,128]{2,1,0:T(8,128)(2,1)}, u32[]{:S(2)}, u32[]{:S(2)}) collective-permute-start(bf16[64,16,128]{2,1,0:T(8,128)(2,1)} %shard_map.73.refs_0_), channel_id=1, source_target_pairs={{0,1},{1,0},{2,3},{3,2},{4,5},{5,4},{6,7},{7,6},{8,9},{9,8},{10,11... | collective-permute-start | bytes 786440 | tf_op jit(solution)/shard_map/ppermute | solution.py:16
  92.4 21.4 %collective-permute-done.mirror_ref = bf16[64,16,512]{2,1,0:T(8,128)(2,1)S(1)} collective-permute-done((bf16[64,16,512]{2,1,0:T(8,128)(2,1)S(1)}, bf16[64,16,512]{2,1,0:T(8,128)(2,1)S(1)}, u32[]{:S(2)}, u32[]{:S(2)}) %collective-permute-start) | collective-permute-done | bytes 1048608 | tf_op jit(solution)/shard_map/ppermute | solution.py:16
  113.8 2.2 %copy-done.6 = bf16[64,16,2048]{2,1,0:T(8,128)(2,1)S(1)} copy-done((bf16[64,16,2048]{2,1,0:T(8,128)(2,1)S(1)}, bf16[64,16,2048]{2,1,0:T(8,128)(2,1)}, u32[]{:S(2)}) %copy-start.6) | copy-done | bytes 4194328
  116.0 4.5 %shard_map.69.refs_5_ = bf16[512,2048]{1,0:T(8,128)(2,1)S(1)} custom-call(bf16[64,16,512]{2,1,0:T(8,128)(2,1)S(1)} %shard_map.68.own_ref, bf16[64,16,512]{2,1,0:T(8,128)(2,1)S(1)} %collective-permute-done.mirror_ref, bf16[64,16,2048]{2,1,0:T(8,128)(2,1)S(1)} %copy-done.2, bf16[64,16,2048]{2,1,0:T(8,128)(2,1)S(1)} %copy-done.6), custom_call_target="tpu_custom_call" | custom-call | flops 4294967296 | bytes 16777216 | tf_op jit(solution)/shard_map/pallas_call | solution.py:105
  120.5 1.3 copy-done.13
  121.9 3.8 %all-to-all-done.1.received_ref = bf16[128,16,384]{2,1,0:T(8,128)(2,1)S(1)} async-done(((bf16[128,16,384]{2,1,0:T(8,128)(2,1)}), bf16[128,16,384]{2,1,0:T(8,128)(2,1)S(1)}, u32[]{:S(2)}, u32[]{:S(2)}) %all-to-all-start.1) | async-done | bytes 1572896 | tf_op jit(solution)/shard_map/all_to_all | solution.py:226
  127.2 2.2 %collective-permute-start.1 = (bf16[64,16,128]{2,1,0:T(8,128)(2,1)S(1)}, bf16[64,16,128]{2,1,0:T(8,128)(2,1)S(1)}, u32[]{:S(2)}, u32[]{:S(2)}) collective-permute-start(bf16[64,16,128]{2,1,0:T(8,128)(2,1)S(1)} %shard_map.70.refs_0_), channel_id=1, source_target_pairs={{0,1},{1,0},{2,3},{3,2},{4,5},{5,4},{6,7},{7,6},{8,9},{9,8},{10,11... | collective-permute-start | bytes 786440 | tf_op jit(solution)/shard_map/ppermute | solution.py:16
  129.5 2.2 %copy-done.3 = bf16[64,16,2048]{2,1,0:T(8,128)(2,1)S(1)} copy-done((bf16[64,16,2048]{2,1,0:T(8,128)(2,1)S(1)}, bf16[64,16,2048]{2,1,0:T(8,128)(2,1)}, u32[]{:S(2)}) %copy-start.3) | copy-done | bytes 4194328
  131.6 2.2 %copy-done.7 = bf16[64,16,2048]{2,1,0:T(8,128)(2,1)S(1)} copy-done((bf16[64,16,2048]{2,1,0:T(8,128)(2,1)S(1)}, bf16[64,16,2048]{2,1,0:T(8,128)(2,1)}, u32[]{:S(2)}) %copy-start.7) | copy-done | bytes 4194328
  133.8 5.6 %shard_map.74.refs_6_ = bf16[1024,2048]{1,0:T(8,128)(2,1)S(1)} custom-call(bf16[64,16,128]{2,1,0:T(8,128)(2,1)} %shard_map.73.refs_0_, bf16[64,16,128]{2,1,0:T(8,128)(2,1)} %collective-permute-done.3.refs_1_, bf16[1024,640]{1,0:T(8,128)(2,1)S(1)} %copy-done.10, bf16[64,16,2048]{2,1,0:T(8,128)(2,1)S(1)} %copy-done.3, bf16[64,16,2048]{2,1,0:T(8,128)(2,1)S(1)} %copy-done.7, ...), custom_call_target="tpu_custom_call" | custom-call | flops 3758096384 | bytes 16777216 | tf_op jit(solution)/shard_map/pallas_call | solution.py:150
  139.4 1.9 %collective-permute-done.2.mirror_ref = bf16[64,16,256]{2,1,0:T(8,128)(2,1)S(1)} collective-permute-done((bf16[64,16,256]{2,1,0:T(8,128)(2,1)S(1)}, bf16[64,16,256]{2,1,0:T(8,128)(2,1)S(1)}, u32[]{:S(2)}, u32[]{:S(2)}) %collective-permute-start.2) | collective-permute-done | bytes 524320 | tf_op jit(solution)/shard_map/ppermute | solution.py:16
  141.3 2.4 %shard_map.72.refs_5_ = bf16[256,2048]{1,0:T(8,128)(2,1)S(1)} custom-call(bf16[64,16,256]{2,1,0:T(8,128)(2,1)S(1)} %shard_map.71.own_ref, bf16[64,16,256]{2,1,0:T(8,128)(2,1)S(1)} %collective-permute-done.2.mirror_ref, bf16[64,16,2048]{2,1,0:T(8,128)(2,1)S(1)} %copy-done.3, bf16[64,16,2048]{2,1,0:T(8,128)(2,1)S(1)} %copy-done.7), custom_call_target="tpu_custom_call" | custom-call | flops 2147483648 | bytes 16777216 | tf_op jit(solution)/shard_map/pallas_call | solution.py:105
  143.7 1.2 collective-permute-done.1.refs_1_
  144.9 4.5 %shard_map.75 = bf16[1024,2048]{1,0:T(8,128)(2,1)} custom-call(bf16[64,16,128]{2,1,0:T(8,128)(2,1)S(1)} %shard_map.70.refs_0_, bf16[64,16,128]{2,1,0:T(8,128)(2,1)S(1)} %collective-permute-done.1.refs_1_, bf16[1024,384]{1,0:T(8,128)(2,1)S(1)} %compare_convert_fusion.1.refs_2_, bf16[64,16,2048]{2,1,0:T(8,128)(2,1)S(1)} %copy-done.4, ...), custom_call_target="tpu_custom_call" | custom-call | flops 2684354560 | bytes 16777216 | tf_op jit(solution)/shard_map/pallas_call | solution.py:150
  (44 shorter events, 5.1 us)
Async XLA Ops:
  0.0 2.0 %copy-start = (bf16[32,16,1024]{2,1,0:T(8,128)(2,1)S(1)}, bf16[32,16,1024]{2,1,0:T(8,128)(2,1)}, u32[]{:S(2)}) copy-start(bf16[32,16,1024]{2,1,0:T(8,128)(2,1)} %param.6) | copy-start | bytes 3145732
  3.9 1.5 %copy-start.8 = (bf16[128,16,640]{2,1,0:T(8,128)(2,1)}, bf16[128,16,640]{2,1,0:T(8,128)(2,1)S(1)}, u32[]{:S(2)}) copy-start(bf16[128,16,640]{2,1,0:T(8,128)(2,1)S(1)} %shard_map.67) | copy-start | bytes 7864324
  5.4 12.3 %copy-start.15 = (s32[64]{0:T(128)S(1)}, s32[64]{0:T(128)}, u32[]{:S(2)}) copy-start(s32[64]{0:T(128)} %param.11) | copy-start | bytes 772
  5.4 74.7 %all-to-all-start = ((bf16[128,16,640]{2,1,0:T(8,128)(2,1)}), bf16[128,16,640]{2,1,0:T(8,128)(2,1)}, u32[]{:S(2)}, u32[]{:S(2)}) async-start(bf16[128,16,640]{2,1,0:T(8,128)(2,1)} %copy-done.8), calls=%async_computation | async-start | bytes 5242880 | tf_op jit(solution)/shard_map/all_to_all | solution.py:219
  22.5 2.2 %copy-start.11 = (bf16[1,64,16,2048]{3,2,1,0:T(8,128)(2,1)S(1)}, bf16[1,64,16,2048]{3,2,1,0:T(8,128)(2,1)}, u32[]{:S(2)}) copy-start(bf16[1,64,16,2048]{3,2,1,0:T(8,128)(2,1)} %param.7) | copy-start | bytes 12582916
  24.7 3.7 %copy-start.12 = (bf16[1,64,16,2048]{3,2,1,0:T(8,128)(2,1)S(1)}, bf16[1,64,16,2048]{3,2,1,0:T(8,128)(2,1)}, u32[]{:S(2)}) copy-start(bf16[1,64,16,2048]{3,2,1,0:T(8,128)(2,1)} %param.8) | copy-start | bytes 12582916
  25.0 2.1 %copy-start.1 = (bf16[64,16,2048]{2,1,0:T(8,128)(2,1)}, bf16[64,16,2048]{2,1,0:T(8,128)(2,1)S(1)}, u32[]{:S(2)}) copy-start(bf16[64,16,2048]{2,1,0:T(8,128)(2,1)S(1)} %shard_map.64.plus_ref.refs_3_) | copy-start | bytes 12582916
  28.7 2.0 %copy-start.5 = (bf16[64,16,2048]{2,1,0:T(8,128)(2,1)}, bf16[64,16,2048]{2,1,0:T(8,128)(2,1)S(1)}, u32[]{:S(2)}) copy-start(bf16[64,16,2048]{2,1,0:T(8,128)(2,1)S(1)} %shard_map.65.minus_ref.refs_4_) | copy-start | bytes 12582916
  31.4 1.1 copy-start.9
  80.2 45.5 %all-to-all-start.1 = ((bf16[128,16,384]{2,1,0:T(8,128)(2,1)}), bf16[128,16,384]{2,1,0:T(8,128)(2,1)S(1)}, u32[]{:S(2)}, u32[]{:S(2)}) async-start(bf16[128,16,384]{2,1,0:T(8,128)(2,1)} %copy-done.9), calls=%async_computation.1 | async-start | bytes 3145728 | tf_op jit(solution)/shard_map/all_to_all | solution.py:226
  85.6 28.2 %copy-start.2 = (bf16[64,16,2048]{2,1,0:T(8,128)(2,1)S(1)}, bf16[64,16,2048]{2,1,0:T(8,128)(2,1)}, u32[]{:S(2)}) copy-start(bf16[64,16,2048]{2,1,0:T(8,128)(2,1)} %copy-done.1) | copy-start | bytes 12582916
  87.7 26.1 %collective-permute-start = (bf16[64,16,512]{2,1,0:T(8,128)(2,1)S(1)}, bf16[64,16,512]{2,1,0:T(8,128)(2,1)S(1)}, u32[]{:S(2)}, u32[]{:S(2)}) collective-permute-start(bf16[64,16,512]{2,1,0:T(8,128)(2,1)S(1)} %shard_map.68.own_ref), channel_id=1, source_target_pairs={{0,1},{1,0},{2,3},{3,2},{4,5},{5,4},{6,7},{7,6},{8,9},{9,8},{10,11... | collective-permute-start | bytes 3145736 | tf_op jit(solution)/shard_map/ppermute | solution.py:16
  90.5 39.0 %collective-permute-start.3 = (bf16[64,16,128]{2,1,0:T(8,128)(2,1)}, bf16[64,16,128]{2,1,0:T(8,128)(2,1)}, u32[]{:S(2)}, u32[]{:S(2)}) collective-permute-start(bf16[64,16,128]{2,1,0:T(8,128)(2,1)} %shard_map.73.refs_0_), channel_id=1, source_target_pairs={{0,1},{1,0},{2,3},{3,2},{4,5},{5,4},{6,7},{7,6},{8,9},{9,8},{10,11... | collective-permute-start | bytes 786440 | tf_op jit(solution)/shard_map/ppermute | solution.py:16
  113.8 2.2 %copy-start.6 = (bf16[64,16,2048]{2,1,0:T(8,128)(2,1)S(1)}, bf16[64,16,2048]{2,1,0:T(8,128)(2,1)}, u32[]{:S(2)}) copy-start(bf16[64,16,2048]{2,1,0:T(8,128)(2,1)} %copy-done.5) | copy-start | bytes 12582916
  120.5 1.4 copy-start.13
  125.7 3.8 %copy-start.10 = (bf16[1024,640]{1,0:T(8,128)(2,1)S(1)}, bf16[1024,640]{1,0:T(8,128)(2,1)}, u32[]{:S(2)}) copy-start(bf16[1024,640]{1,0:T(8,128)(2,1)} %compare_convert_fusion.refs_2_) | copy-start | bytes 3932164
  125.7 3.8 %copy-start.14 = (bf16[512,2048]{1,0:T(8,128)(2,1)S(1)}, bf16[512,2048]{1,0:T(8,128)(2,1)}, u32[]{:S(2)}) copy-start(bf16[512,2048]{1,0:T(8,128)(2,1)} %copy-done.13) | copy-start | bytes 6291460
  126.4 14.9 %collective-permute-start.2 = (bf16[64,16,256]{2,1,0:T(8,128)(2,1)S(1)}, bf16[64,16,256]{2,1,0:T(8,128)(2,1)S(1)}, u32[]{:S(2)}, u32[]{:S(2)}) collective-permute-start(bf16[64,16,256]{2,1,0:T(8,128)(2,1)S(1)} %shard_map.71.own_ref), channel_id=1, source_target_pairs={{0,1},{1,0},{2,3},{3,2},{4,5},{5,4},{6,7},{7,6},{8,9},{9,8},{10,11... | collective-permute-start | bytes 1572872 | tf_op jit(solution)/shard_map/ppermute | solution.py:16
  127.2 17.7 %collective-permute-start.1 = (bf16[64,16,128]{2,1,0:T(8,128)(2,1)S(1)}, bf16[64,16,128]{2,1,0:T(8,128)(2,1)S(1)}, u32[]{:S(2)}, u32[]{:S(2)}) collective-permute-start(bf16[64,16,128]{2,1,0:T(8,128)(2,1)S(1)} %shard_map.70.refs_0_), channel_id=1, source_target_pairs={{0,1},{1,0},{2,3},{3,2},{4,5},{5,4},{6,7},{7,6},{8,9},{9,8},{10,11... | collective-permute-start | bytes 786440 | tf_op jit(solution)/shard_map/ppermute | solution.py:16
  129.4 2.2 %copy-start.3 = (bf16[64,16,2048]{2,1,0:T(8,128)(2,1)S(1)}, bf16[64,16,2048]{2,1,0:T(8,128)(2,1)}, u32[]{:S(2)}) copy-start(bf16[64,16,2048]{2,1,0:T(8,128)(2,1)} %copy-done.1) | copy-start | bytes 12582916
  131.6 2.2 %copy-start.7 = (bf16[64,16,2048]{2,1,0:T(8,128)(2,1)S(1)}, bf16[64,16,2048]{2,1,0:T(8,128)(2,1)}, u32[]{:S(2)}) copy-start(bf16[64,16,2048]{2,1,0:T(8,128)(2,1)} %copy-done.5) | copy-start | bytes 12582916
  141.3 3.6 %copy-start.4 = (bf16[64,16,2048]{2,1,0:T(8,128)(2,1)S(1)}, bf16[64,16,2048]{2,1,0:T(8,128)(2,1)}, u32[]{:S(2)}) copy-start(bf16[64,16,2048]{2,1,0:T(8,128)(2,1)} %copy-done.1) | copy-start | bytes 12582916

commit v4 on v3

--- a/solution.py
+++ b/solution.py
@@ -7,7 +7,7 @@
 from jax.experimental.pallas import tpu as pltpu
 from jax.sharding import PartitionSpec as P
 
-CHUNKS = ((512, 128), (256, 128))
+CHUNKS = ((384, 256), (256, 128))
 BLOCK = 512
 VMEM_LIMIT = 20 * 1024 * 1024
 

time: 150 us -> 150 us (level)
    ppermute x4, waiting for transfers between devices: 24.5 us -> 17.5 us  [mirror_pair(): lax.ppermute(x, 'pair', [(i, i ^ 1) for i in range(lax.axis_size('pair'))])]
    all_to_all x1, waiting for transfers between devices: 3.79 us -> 10.6 us  [body(): landed.append(lax.all_to_all(outgoing, 'tiles', 0, 0, tiled=True))]
where the time goes in v4:
time: 150 us
  waiting for transfers between devices  75.8 us (51%)
  Pallas kernels  25.3 us (17%)
  starting transfers between devices  22.2 us (15%)
  local copies, waits for them, and re-layouts  19 us (13%)
  other arithmetic  4.8 us (3%)
  matrix products  1.96 us (1%)
    all_to_all x1, waiting for transfers between devices, body(): landed = [lax.all_to_all(pack(send, chunks[0]), 'tiles', 0, 0, tiled=True)]  47.7 us
    unnamed x32, local copies, waits for them, and re-layouts  18 us
    ppermute x4, waiting for transfers between devices, mirror_pair(): lax.ppermute(x, 'pair', [(i, i ^ 1) for i in range(lax.axis_size('pair'))])  17.5 us
    all_to_all x1, starting transfers between devices, body(): landed = [lax.all_to_all(pack(send, chunks[0]), 'tiles', 0, 0, tiled=True)]  12.3 us
    pallas_call x2, Pallas kernels, finish(): pl.pallas_call(functools.partial(finish_kernel, len(earlier), base is not...  11.3 us
    all_to_all x1, waiting for transfers between devices, body(): landed.append(lax.all_to_all(outgoing, 'tiles', 0, 0, tiled=True))  10.6 us
    pallas_call x4, Pallas kernels, unpack(): pl.pallas_call(functools.partial(window_kernel, begin), out_shape=jax.Sha...  6.13 us
    pallas_call x2, Pallas kernels, make_rows(): pl.pallas_call(rows_kernel, out_shape=jax.ShapeDtypeStruct((own.shape[2],...  5.82 us
  transfers between devices with their start and end apart: 6, of which 5 were waited for; matrix products, arithmetic and copies ran while one was open for 3% of the time, Pallas kernels for 13%

profile of v4, /device:TPU:28, one launch (start us, length us, event | category | flops | bytes accessed | tf_op | source)
XLA Modules:
  0.0 149.5 jit_solution(3013039890795905304)
XLA Ops:
  0.0 1.0 select_reduce_fusion.1
  1.3 0.7 iota_select_fusion
  2.0 1.1 fusion.2
  3.1 0.8 shard_map.67
  3.9 1.5 %copy-done.8 = bf16[128,16,640]{2,1,0:T(8,128)(2,1)} copy-done((bf16[128,16,640]{2,1,0:T(8,128)(2,1)}, bf16[128,16,640]{2,1,0:T(8,128)(2,1)S(1)}, u32[]{:S(2)}) %copy-start.8) | copy-done | bytes 2621464
  5.4 12.3 %all-to-all-start = ((bf16[128,16,640]{2,1,0:T(8,128)(2,1)}), bf16[128,16,640]{2,1,0:T(8,128)(2,1)}, u32[]{:S(2)}, u32[]{:S(2)}) async-start(bf16[128,16,640]{2,1,0:T(8,128)(2,1)} %copy-done.8), calls=%async_computation | async-start | bytes 5242880 | tf_op jit(solution)/shard_map/all_to_all | solution.py:219
  18.4 0.8 fusion.7
  21.2 1.4 compare_convert_fusion.refs_2_
  22.5 2.2 %copy-done.10 = bf16[1,64,16,2048]{3,2,1,0:T(8,128)(2,1)S(1)} copy-done((bf16[1,64,16,2048]{3,2,1,0:T(8,128)(2,1)S(1)}, bf16[1,64,16,2048]{3,2,1,0:T(8,128)(2,1)}, u32[]{:S(2)}) %copy-start.10) | copy-done | bytes 4194328
  25.0 2.1 %copy-done.1 = bf16[64,16,2048]{2,1,0:T(8,128)(2,1)} copy-done((bf16[64,16,2048]{2,1,0:T(8,128)(2,1)}, bf16[64,16,2048]{2,1,0:T(8,128)(2,1)S(1)}, u32[]{:S(2)}) %copy-start.1) | copy-done | bytes 4194328
  27.1 1.3 copy-done.11
  28.7 2.0 %copy-done.5 = bf16[64,16,2048]{2,1,0:T(8,128)(2,1)} copy-done((bf16[64,16,2048]{2,1,0:T(8,128)(2,1)}, bf16[64,16,2048]{2,1,0:T(8,128)(2,1)S(1)}, u32[]{:S(2)}) %copy-start.5) | copy-done | bytes 4194328
  30.7 0.7 shard_map.66
  31.4 1.1 copy-done.9
  32.5 47.7 %all-to-all-done.received_ref = bf16[128,16,640]{2,1,0:T(8,128)(2,1)} async-done(((bf16[128,16,640]{2,1,0:T(8,128)(2,1)}), bf16[128,16,640]{2,1,0:T(8,128)(2,1)}, u32[]{:S(2)}, u32[]{:S(2)}) %all-to-all-start) | async-done | bytes 2621472 | tf_op jit(solution)/shard_map/all_to_all | solution.py:219
  80.2 5.4 %all-to-all-start.1 = ((bf16[128,16,384]{2,1,0:T(8,128)(2,1)}), bf16[128,16,384]{2,1,0:T(8,128)(2,1)S(1)}, u32[]{:S(2)}, u32[]{:S(2)}) async-start(bf16[128,16,384]{2,1,0:T(8,128)(2,1)} %copy-done.9), calls=%async_computation.1 | async-start | bytes 3145728 | tf_op jit(solution)/shard_map/all_to_all | solution.py:226
  85.6 2.1 %shard_map.68.own_ref = bf16[64,16,384]{2,1,0:T(8,128)(2,1)S(1)} custom-call(s32[64]{0:T(128)S(1)} %add_select_fusion.where_ref, bf16[128,16,640]{2,1,0:T(8,128)(2,1)} %all-to-all-done.received_ref), custom_call_target="tpu_custom_call" | custom-call | tf_op jit(solution)/shard_map/pallas_call | solution.py:57
  87.9 2.7 %shard_map.73.refs_0_ = bf16[64,16,256]{2,1,0:T(8,128)(2,1)} custom-call(s32[64]{0:T(128)S(1)} %add_select_fusion.where_ref, bf16[128,16,640]{2,1,0:T(8,128)(2,1)} %all-to-all-done.received_ref), custom_call_target="tpu_custom_call" | custom-call | tf_op jit(solution)/shard_map/pallas_call | solution.py:57
  90.6 1.9 %collective-permute-start.3 = (bf16[64,16,256]{2,1,0:T(8,128)(2,1)}, bf16[64,16,256]{2,1,0:T(8,128)(2,1)}, u32[]{:S(2)}, u32[]{:S(2)}) collective-permute-start(bf16[64,16,256]{2,1,0:T(8,128)(2,1)} %shard_map.73.refs_0_), channel_id=1, source_target_pairs={{0,1},{1,0},{2,3},{3,2},{4,5},{5,4},{6,7},{7,6},{8,9},{9,8},{10,11... | collective-permute-start | bytes 1572872 | tf_op jit(solution)/shard_map/ppermute | solution.py:16
  92.5 15.7 %collective-permute-done.mirror_ref = bf16[64,16,384]{2,1,0:T(8,128)(2,1)S(1)} collective-permute-done((bf16[64,16,384]{2,1,0:T(8,128)(2,1)S(1)}, bf16[64,16,384]{2,1,0:T(8,128)(2,1)S(1)}, u32[]{:S(2)}, u32[]{:S(2)}) %collective-permute-start) | collective-permute-done | bytes 786464 | tf_op jit(solution)/shard_map/ppermute | solution.py:16
  108.2 2.2 %copy-done.6 = bf16[64,16,2048]{2,1,0:T(8,128)(2,1)S(1)} copy-done((bf16[64,16,2048]{2,1,0:T(8,128)(2,1)S(1)}, bf16[64,16,2048]{2,1,0:T(8,128)(2,1)}, u32[]{:S(2)}) %copy-start.6) | copy-done | bytes 4194328
  110.4 3.5 %shard_map.69.refs_5_ = bf16[384,2048]{1,0:T(8,128)(2,1)S(1)} custom-call(bf16[64,16,384]{2,1,0:T(8,128)(2,1)S(1)} %shard_map.68.own_ref, bf16[64,16,384]{2,1,0:T(8,128)(2,1)S(1)} %collective-permute-done.mirror_ref, bf16[64,16,2048]{2,1,0:T(8,128)(2,1)S(1)} %copy-done.2, bf16[64,16,2048]{2,1,0:T(8,128)(2,1)S(1)} %copy-done.6), custom_call_target="tpu_custom_call" | custom-call | flops 3221225472 | bytes 16777216 | tf_op jit(solution)/shard_map/pallas_call | solution.py:105
  113.9 1.2 copy-done.13
  115.1 10.6 %all-to-all-done.1.received_ref = bf16[128,16,384]{2,1,0:T(8,128)(2,1)S(1)} async-done(((bf16[128,16,384]{2,1,0:T(8,128)(2,1)}), bf16[128,16,384]{2,1,0:T(8,128)(2,1)S(1)}, u32[]{:S(2)}, u32[]{:S(2)}) %all-to-all-start.1) | async-done | bytes 1572896 | tf_op jit(solution)/shard_map/all_to_all | solution.py:226
  126.5 0.7 shard_map.70.refs_0_
  127.2 2.2 %collective-permute-start.1 = (bf16[64,16,128]{2,1,0:T(8,128)(2,1)S(1)}, bf16[64,16,128]{2,1,0:T(8,128)(2,1)S(1)}, u32[]{:S(2)}, u32[]{:S(2)}) collective-permute-start(bf16[64,16,128]{2,1,0:T(8,128)(2,1)S(1)} %shard_map.70.refs_0_), channel_id=1, source_target_pairs={{0,1},{1,0},{2,3},{3,2},{4,5},{5,4},{6,7},{7,6},{8,9},{9,8},{10,11... | collective-permute-start | bytes 786440 | tf_op jit(solution)/shard_map/ppermute | solution.py:16
  129.5 2.2 %copy-done.3 = bf16[64,16,2048]{2,1,0:T(8,128)(2,1)S(1)} copy-done((bf16[64,16,2048]{2,1,0:T(8,128)(2,1)S(1)}, bf16[64,16,2048]{2,1,0:T(8,128)(2,1)}, u32[]{:S(2)}) %copy-start.3) | copy-done | bytes 4194328
  131.6 2.2 %copy-done.7 = bf16[64,16,2048]{2,1,0:T(8,128)(2,1)S(1)} copy-done((bf16[64,16,2048]{2,1,0:T(8,128)(2,1)S(1)}, bf16[64,16,2048]{2,1,0:T(8,128)(2,1)}, u32[]{:S(2)}) %copy-start.7) | copy-done | bytes 4194328
  133.8 6.8 %shard_map.74.refs_6_ = bf16[1024,2048]{1,0:T(8,128)(2,1)S(1)} custom-call(bf16[64,16,256]{2,1,0:T(8,128)(2,1)} %shard_map.73.refs_0_, bf16[64,16,256]{2,1,0:T(8,128)(2,1)} %collective-permute-done.3.refs_1_, bf16[1024,640]{1,0:T(8,128)(2,1)S(1)} %copy-done.12, bf16[64,16,2048]{2,1,0:T(8,128)(2,1)S(1)} %copy-done.3, bf16[64,16,2048]{2,1,0:T(8,128)(2,1)S(1)} %copy-done.7, ...), custom_call_target="tpu_custom_call" | custom-call | flops 4831838208 | bytes 16777216 | tf_op jit(solution)/shard_map/pallas_call | solution.py:150
  141.3 2.4 %shard_map.72.refs_5_ = bf16[256,2048]{1,0:T(8,128)(2,1)S(1)} custom-call(bf16[64,16,256]{2,1,0:T(8,128)(2,1)S(1)} %shard_map.71.own_ref, bf16[64,16,256]{2,1,0:T(8,128)(2,1)S(1)} %collective-permute-done.2.mirror_ref, bf16[64,16,2048]{2,1,0:T(8,128)(2,1)S(1)} %copy-done.3, bf16[64,16,2048]{2,1,0:T(8,128)(2,1)S(1)} %copy-done.7), custom_call_target="tpu_custom_call" | custom-call | flops 2147483648 | bytes 16777216 | tf_op jit(solution)/shard_map/pallas_call | solution.py:105
  143.7 1.2 collective-permute-done.1.refs_1_
  144.9 4.5 %shard_map.75 = bf16[1024,2048]{1,0:T(8,128)(2,1)} custom-call(bf16[64,16,128]{2,1,0:T(8,128)(2,1)S(1)} %shard_map.70.refs_0_, bf16[64,16,128]{2,1,0:T(8,128)(2,1)S(1)} %collective-permute-done.1.refs_1_, bf16[1024,384]{1,0:T(8,128)(2,1)S(1)} %compare_convert_fusion.1.refs_2_, bf16[64,16,2048]{2,1,0:T(8,128)(2,1)S(1)} %copy-done.4, ...), custom_call_target="tpu_custom_call" | custom-call | flops 2684354560 | bytes 16777216 | tf_op jit(solution)/shard_map/pallas_call | solution.py:150
  (44 shorter events, 5.1 us)
Async XLA Ops:
  0.0 2.0 %copy-start = (bf16[32,16,1024]{2,1,0:T(8,128)(2,1)S(1)}, bf16[32,16,1024]{2,1,0:T(8,128)(2,1)}, u32[]{:S(2)}) copy-start(bf16[32,16,1024]{2,1,0:T(8,128)(2,1)} %param.6) | copy-start | bytes 3145732
  3.9 1.5 %copy-start.8 = (bf16[128,16,640]{2,1,0:T(8,128)(2,1)}, bf16[128,16,640]{2,1,0:T(8,128)(2,1)S(1)}, u32[]{:S(2)}) copy-start(bf16[128,16,640]{2,1,0:T(8,128)(2,1)S(1)} %shard_map.67) | copy-start | bytes 7864324
  5.4 12.3 %copy-start.15 = (s32[64]{0:T(128)S(1)}, s32[64]{0:T(128)}, u32[]{:S(2)}) copy-start(s32[64]{0:T(128)} %param.11) | copy-start | bytes 772
  5.4 74.7 %all-to-all-start = ((bf16[128,16,640]{2,1,0:T(8,128)(2,1)}), bf16[128,16,640]{2,1,0:T(8,128)(2,1)}, u32[]{:S(2)}, u32[]{:S(2)}) async-start(bf16[128,16,640]{2,1,0:T(8,128)(2,1)} %copy-done.8), calls=%async_computation | async-start | bytes 5242880 | tf_op jit(solution)/shard_map/all_to_all | solution.py:219
  22.5 2.2 %copy-start.10 = (bf16[1,64,16,2048]{3,2,1,0:T(8,128)(2,1)S(1)}, bf16[1,64,16,2048]{3,2,1,0:T(8,128)(2,1)}, u32[]{:S(2)}) copy-start(bf16[1,64,16,2048]{3,2,1,0:T(8,128)(2,1)} %param.7) | copy-start | bytes 12582916
  24.7 3.7 %copy-start.11 = (bf16[1,64,16,2048]{3,2,1,0:T(8,128)(2,1)S(1)}, bf16[1,64,16,2048]{3,2,1,0:T(8,128)(2,1)}, u32[]{:S(2)}) copy-start(bf16[1,64,16,2048]{3,2,1,0:T(8,128)(2,1)} %param.8) | copy-start | bytes 12582916
  25.0 2.1 %copy-start.1 = (bf16[64,16,2048]{2,1,0:T(8,128)(2,1)}, bf16[64,16,2048]{2,1,0:T(8,128)(2,1)S(1)}, u32[]{:S(2)}) copy-start(bf16[64,16,2048]{2,1,0:T(8,128)(2,1)S(1)} %shard_map.64.plus_ref.refs_3_) | copy-start | bytes 12582916
  28.7 2.0 %copy-start.5 = (bf16[64,16,2048]{2,1,0:T(8,128)(2,1)}, bf16[64,16,2048]{2,1,0:T(8,128)(2,1)S(1)}, u32[]{:S(2)}) copy-start(bf16[64,16,2048]{2,1,0:T(8,128)(2,1)S(1)} %shard_map.65.minus_ref.refs_4_) | copy-start | bytes 12582916
  31.4 1.1 copy-start.9
  80.2 45.5 %all-to-all-start.1 = ((bf16[128,16,384]{2,1,0:T(8,128)(2,1)}), bf16[128,16,384]{2,1,0:T(8,128)(2,1)S(1)}, u32[]{:S(2)}, u32[]{:S(2)}) async-start(bf16[128,16,384]{2,1,0:T(8,128)(2,1)} %copy-done.9), calls=%async_computation.1 | async-start | bytes 3145728 | tf_op jit(solution)/shard_map/all_to_all | solution.py:226
  85.6 22.6 %copy-start.2 = (bf16[64,16,2048]{2,1,0:T(8,128)(2,1)S(1)}, bf16[64,16,2048]{2,1,0:T(8,128)(2,1)}, u32[]{:S(2)}) copy-start(bf16[64,16,2048]{2,1,0:T(8,128)(2,1)} %copy-done.1) | copy-start | bytes 12582916
  87.7 20.5 %collective-permute-start = (bf16[64,16,384]{2,1,0:T(8,128)(2,1)S(1)}, bf16[64,16,384]{2,1,0:T(8,128)(2,1)S(1)}, u32[]{:S(2)}, u32[]{:S(2)}) collective-permute-start(bf16[64,16,384]{2,1,0:T(8,128)(2,1)S(1)} %shard_map.68.own_ref), channel_id=1, source_target_pairs={{0,1},{1,0},{2,3},{3,2},{4,5},{5,4},{6,7},{7,6},{8,9},{9,8},{10,11... | collective-permute-start | bytes 2359304 | tf_op jit(solution)/shard_map/ppermute | solution.py:16
  90.6 38.9 %collective-permute-start.3 = (bf16[64,16,256]{2,1,0:T(8,128)(2,1)}, bf16[64,16,256]{2,1,0:T(8,128)(2,1)}, u32[]{:S(2)}, u32[]{:S(2)}) collective-permute-start(bf16[64,16,256]{2,1,0:T(8,128)(2,1)} %shard_map.73.refs_0_), channel_id=1, source_target_pairs={{0,1},{1,0},{2,3},{3,2},{4,5},{5,4},{6,7},{7,6},{8,9},{9,8},{10,11... | collective-permute-start | bytes 1572872 | tf_op jit(solution)/shard_map/ppermute | solution.py:16
  108.2 2.2 %copy-start.6 = (bf16[64,16,2048]{2,1,0:T(8,128)(2,1)S(1)}, bf16[64,16,2048]{2,1,0:T(8,128)(2,1)}, u32[]{:S(2)}) copy-start(bf16[64,16,2048]{2,1,0:T(8,128)(2,1)} %copy-done.5) | copy-start | bytes 12582916
  113.9 1.2 copy-start.13
  125.7 3.8 %copy-start.12 = (bf16[1024,640]{1,0:T(8,128)(2,1)S(1)}, bf16[1024,640]{1,0:T(8,128)(2,1)}, u32[]{:S(2)}) copy-start(bf16[1024,640]{1,0:T(8,128)(2,1)} %compare_convert_fusion.refs_2_) | copy-start | bytes 3932164
  125.7 3.8 %copy-start.14 = (bf16[384,2048]{1,0:T(8,128)(2,1)S(1)}, bf16[384,2048]{1,0:T(8,128)(2,1)}, u32[]{:S(2)}) copy-start(bf16[384,2048]{1,0:T(8,128)(2,1)} %copy-done.13) | copy-start | bytes 4718596
  126.4 14.9 %collective-permute-start.2 = (bf16[64,16,256]{2,1,0:T(8,128)(2,1)S(1)}, bf16[64,16,256]{2,1,0:T(8,128)(2,1)S(1)}, u32[]{:S(2)}, u32[]{:S(2)}) collective-permute-start(bf16[64,16,256]{2,1,0:T(8,128)(2,1)S(1)} %shard_map.71.own_ref), channel_id=1, source_target_pairs={{0,1},{1,0},{2,3},{3,2},{4,5},{5,4},{6,7},{7,6},{8,9},{9,8},{10,11... | collective-permute-start | bytes 1572872 | tf_op jit(solution)/shard_map/ppermute | solution.py:16
  127.2 17.7 %collective-permute-start.1 = (bf16[64,16,128]{2,1,0:T(8,128)(2,1)S(1)}, bf16[64,16,128]{2,1,0:T(8,128)(2,1)S(1)}, u32[]{:S(2)}, u32[]{:S(2)}) collective-permute-start(bf16[64,16,128]{2,1,0:T(8,128)(2,1)S(1)} %shard_map.70.refs_0_), channel_id=1, source_target_pairs={{0,1},{1,0},{2,3},{3,2},{4,5},{5,4},{6,7},{7,6},{8,9},{9,8},{10,11... | collective-permute-start | bytes 786440 | tf_op jit(solution)/shard_map/ppermute | solution.py:16
  129.4 2.2 %copy-start.3 = (bf16[64,16,2048]{2,1,0:T(8,128)(2,1)S(1)}, bf16[64,16,2048]{2,1,0:T(8,128)(2,1)}, u32[]{:S(2)}) copy-start(bf16[64,16,2048]{2,1,0:T(8,128)(2,1)} %copy-done.1) | copy-start | bytes 12582916
  131.6 2.2 %copy-start.7 = (bf16[64,16,2048]{2,1,0:T(8,128)(2,1)S(1)}, bf16[64,16,2048]{2,1,0:T(8,128)(2,1)}, u32[]{:S(2)}) copy-start(bf16[64,16,2048]{2,1,0:T(8,128)(2,1)} %copy-done.5) | copy-start | bytes 12582916
  141.3 3.6 %copy-start.4 = (bf16[64,16,2048]{2,1,0:T(8,128)(2,1)S(1)}, bf16[64,16,2048]{2,1,0:T(8,128)(2,1)}, u32[]{:S(2)}) copy-start(bf16[64,16,2048]{2,1,0:T(8,128)(2,1)} %copy-done.1) | copy-start | bytes 12582916

commit v5 on v3

--- a/solution.py
+++ b/solution.py
@@ -28,20 +28,21 @@
     return pltpu.CompilerParams(vmem_limit_bytes=VMEM_LIMIT)
 
 
-def pack_kernel(table_ref, tiles_ref, out_ref):
-    for k in range(out_ref.shape[0]):
-        out_ref[k] = tiles_ref[table_ref[k]]
-
-
-def pack(table, tiles):
-    count = table.shape[0]
+def pack_kernel(first_ref, last_ref, tiles_ref, out_ref):
+    for k in range(first_ref.shape[0]):
+        out_ref[2 * k] = tiles_ref[first_ref[k]]
+        out_ref[2 * k + 1] = tiles_ref[last_ref[k]]
+
+
+def pack(tables, tiles):
+    count = 2 * tables[0].shape[0]
     return pl.pallas_call(
         pack_kernel,
         out_shape=jax.ShapeDtypeStruct((count,) + tiles.shape[1:], tiles.dtype),
-        in_specs=scalars() + whole(1),
+        in_specs=scalars() * 2 + whole(1),
         out_specs=whole(1)[0],
         compiler_params=params(),
-    )(table, tiles)
+    )(*tables, tiles)
 
 
 def window_kernel(begin, where_ref, received_ref, out_ref):
@@ -183,7 +184,7 @@
     coded = position[None, :] * 32 + (win_tile & 31)
     first = jnp.min(jnp.where(mine, coded, 1 << 20), axis=1) & 31
     last = jnp.maximum(jnp.max(jnp.where(mine, coded, -1), axis=1), 0) & 31
-    send = jnp.stack([first, last], axis=1).reshape(-1)
+    send = first, last
     own = lax.dynamic_index_in_dim(sources, me, 0, keepdims=False)
     living = position < lax.dynamic_index_in_dim(win_count, me, 0, keepdims=False)
     earlier = (

time: 150 us -> 150 us (level)
  no operation moved by 1% of the time
where the time goes in v5:
time: 150 us; the launch traced here: 149 us
  waiting for transfers between devices  75.9 us (51%)
  Pallas kernels  25.1 us (17%)
  starting transfers between devices  22.2 us (15%)
  local copies, waits for them, and re-layouts  19 us (13%)
  other arithmetic  4.78 us (3%)
  matrix products  1.95 us (1%)
    all_to_all x1, waiting for transfers between devices, body(): landed = [lax.all_to_all(pack(send, chunks[0]), 'tiles', 0, 0, tiled=True)]  47.7 us
    ppermute x4, waiting for transfers between devices, mirror_pair(): lax.ppermute(x, 'pair', [(i, i ^ 1) for i in range(lax.axis_size('pair'))])  24.4 us
    unnamed x32, local copies, waits for them, and re-layouts  18.1 us
    all_to_all x1, starting transfers between devices, body(): landed = [lax.all_to_all(pack(send, chunks[0]), 'tiles', 0, 0, tiled=True)]  12.3 us
    pallas_call x2, Pallas kernels, finish(): pl.pallas_call(functools.partial(finish_kernel, len(earlier), base is not...  10.1 us
    pallas_call x2, Pallas kernels, make_rows(): pl.pallas_call(rows_kernel, out_shape=jax.ShapeDtypeStruct((own.shape[2],...  6.93 us
    pallas_call x4, Pallas kernels, unpack(): pl.pallas_call(functools.partial(window_kernel, begin), out_shape=jax.Sha...  6.04 us
    all_to_all x1, starting transfers between devices, body(): landed.append(lax.all_to_all(outgoing, 'tiles', 0, 0, tiled=True))  5.42 us
  transfers between devices with their start and end apart: 6, of which 5 were waited for; matrix products, arithmetic and copies ran while one was open for 3% of the time, Pallas kernels for 13%

profile of v5, /device:TPU:28, one launch (start us, length us, event | category | flops | bytes accessed | tf_op | source)
XLA Modules:
  0.0 149.3 jit_solution(18026472378335091432)
XLA Ops:
  0.0 0.8 iota_select_fusion
  0.8 0.9 select_reduce_fusion
  1.8 1.1 fusion.2
  2.9 0.8 shard_map.67
  3.7 1.5 %copy-done.8 = bf16[128,16,640]{2,1,0:T(8,128)(2,1)} copy-done((bf16[128,16,640]{2,1,0:T(8,128)(2,1)}, bf16[128,16,640]{2,1,0:T(8,128)(2,1)S(1)}, u32[]{:S(2)}) %copy-start.8) | copy-done | bytes 2621464
  5.2 12.3 %all-to-all-start = ((bf16[128,16,640]{2,1,0:T(8,128)(2,1)}), bf16[128,16,640]{2,1,0:T(8,128)(2,1)}, u32[]{:S(2)}, u32[]{:S(2)}) async-start(bf16[128,16,640]{2,1,0:T(8,128)(2,1)} %copy-done.8), calls=%async_computation | async-start | bytes 5242880 | tf_op jit(solution)/shard_map/all_to_all | solution.py:220
  18.1 0.8 fusion.7
  20.9 1.4 compare_convert_fusion.refs_2_
  22.3 2.2 %copy-done.11 = bf16[1,64,16,2048]{3,2,1,0:T(8,128)(2,1)S(1)} copy-done((bf16[1,64,16,2048]{3,2,1,0:T(8,128)(2,1)S(1)}, bf16[1,64,16,2048]{3,2,1,0:T(8,128)(2,1)}, u32[]{:S(2)}) %copy-start.11) | copy-done | bytes 4194328
  24.8 2.1 %copy-done.1 = bf16[64,16,2048]{2,1,0:T(8,128)(2,1)} copy-done((bf16[64,16,2048]{2,1,0:T(8,128)(2,1)}, bf16[64,16,2048]{2,1,0:T(8,128)(2,1)S(1)}, u32[]{:S(2)}) %copy-start.1) | copy-done | bytes 4194328
  26.9 1.3 copy-done.12
  28.5 2.0 %copy-done.5 = bf16[64,16,2048]{2,1,0:T(8,128)(2,1)} copy-done((bf16[64,16,2048]{2,1,0:T(8,128)(2,1)}, bf16[64,16,2048]{2,1,0:T(8,128)(2,1)S(1)}, u32[]{:S(2)}) %copy-start.5) | copy-done | bytes 4194328
  30.4 0.7 shard_map.66
  31.2 1.1 copy-done.9
  32.3 47.7 %all-to-all-done.received_ref = bf16[128,16,640]{2,1,0:T(8,128)(2,1)} async-done(((bf16[128,16,640]{2,1,0:T(8,128)(2,1)}), bf16[128,16,640]{2,1,0:T(8,128)(2,1)}, u32[]{:S(2)}, u32[]{:S(2)}) %all-to-all-start) | async-done | bytes 2621472 | tf_op jit(solution)/shard_map/all_to_all | solution.py:220
  79.9 5.4 %all-to-all-start.1 = ((bf16[128,16,384]{2,1,0:T(8,128)(2,1)}), bf16[128,16,384]{2,1,0:T(8,128)(2,1)S(1)}, u32[]{:S(2)}, u32[]{:S(2)}) async-start(bf16[128,16,384]{2,1,0:T(8,128)(2,1)} %copy-done.9), calls=%async_computation.1 | async-start | bytes 3145728 | tf_op jit(solution)/shard_map/all_to_all | solution.py:227
  85.4 2.0 %shard_map.68.own_ref = bf16[64,16,512]{2,1,0:T(8,128)(2,1)S(1)} custom-call(s32[64]{0:T(128)S(1)} %add_select_fusion.where_ref, bf16[128,16,640]{2,1,0:T(8,128)(2,1)} %all-to-all-done.received_ref), custom_call_target="tpu_custom_call" | custom-call | tf_op jit(solution)/shard_map/pallas_call | solution.py:58
  87.8 2.6 %shard_map.73.refs_0_ = bf16[64,16,128]{2,1,0:T(8,128)(2,1)} custom-call(s32[64]{0:T(128)S(1)} %add_select_fusion.where_ref, bf16[128,16,640]{2,1,0:T(8,128)(2,1)} %all-to-all-done.received_ref), custom_call_target="tpu_custom_call" | custom-call | tf_op jit(solution)/shard_map/pallas_call | solution.py:58
  90.4 1.8 %collective-permute-start.3 = (bf16[64,16,128]{2,1,0:T(8,128)(2,1)}, bf16[64,16,128]{2,1,0:T(8,128)(2,1)}, u32[]{:S(2)}, u32[]{:S(2)}) collective-permute-start(bf16[64,16,128]{2,1,0:T(8,128)(2,1)} %shard_map.73.refs_0_), channel_id=1, source_target_pairs={{0,1},{1,0},{2,3},{3,2},{4,5},{5,4},{6,7},{7,6},{8,9},{9,8},{10,11... | collective-permute-start | bytes 786440 | tf_op jit(solution)/shard_map/ppermute | solution.py:16
  92.2 21.4 %collective-permute-done.mirror_ref = bf16[64,16,512]{2,1,0:T(8,128)(2,1)S(1)} collective-permute-done((bf16[64,16,512]{2,1,0:T(8,128)(2,1)S(1)}, bf16[64,16,512]{2,1,0:T(8,128)(2,1)S(1)}, u32[]{:S(2)}, u32[]{:S(2)}) %collective-permute-start) | collective-permute-done | bytes 1048608 | tf_op jit(solution)/shard_map/ppermute | solution.py:16
  113.5 2.2 %copy-done.6 = bf16[64,16,2048]{2,1,0:T(8,128)(2,1)S(1)} copy-done((bf16[64,16,2048]{2,1,0:T(8,128)(2,1)S(1)}, bf16[64,16,2048]{2,1,0:T(8,128)(2,1)}, u32[]{:S(2)}) %copy-start.6) | copy-done | bytes 4194328
  115.7 4.6 %shard_map.69.refs_5_ = bf16[512,2048]{1,0:T(8,128)(2,1)S(1)} custom-call(bf16[64,16,512]{2,1,0:T(8,128)(2,1)S(1)} %shard_map.68.own_ref, bf16[64,16,512]{2,1,0:T(8,128)(2,1)S(1)} %collective-permute-done.mirror_ref, bf16[64,16,2048]{2,1,0:T(8,128)(2,1)S(1)} %copy-done.2, bf16[64,16,2048]{2,1,0:T(8,128)(2,1)S(1)} %copy-done.6), custom_call_target="tpu_custom_call" | custom-call | flops 4294967296 | bytes 16777216 | tf_op jit(solution)/shard_map/pallas_call | solution.py:106
  120.3 1.3 copy-done.13
  121.6 3.8 %all-to-all-done.1.received_ref = bf16[128,16,384]{2,1,0:T(8,128)(2,1)S(1)} async-done(((bf16[128,16,384]{2,1,0:T(8,128)(2,1)}), bf16[128,16,384]{2,1,0:T(8,128)(2,1)S(1)}, u32[]{:S(2)}, u32[]{:S(2)}) %all-to-all-start.1) | async-done | bytes 1572896 | tf_op jit(solution)/shard_map/all_to_all | solution.py:227
  127.1 2.1 %collective-permute-start.1 = (bf16[64,16,128]{2,1,0:T(8,128)(2,1)S(1)}, bf16[64,16,128]{2,1,0:T(8,128)(2,1)S(1)}, u32[]{:S(2)}, u32[]{:S(2)}) collective-permute-start(bf16[64,16,128]{2,1,0:T(8,128)(2,1)S(1)} %shard_map.70.refs_0_), channel_id=1, source_target_pairs={{0,1},{1,0},{2,3},{3,2},{4,5},{5,4},{6,7},{7,6},{8,9},{9,8},{10,11... | collective-permute-start | bytes 786440 | tf_op jit(solution)/shard_map/ppermute | solution.py:16
  129.2 2.2 %copy-done.3 = bf16[64,16,2048]{2,1,0:T(8,128)(2,1)S(1)} copy-done((bf16[64,16,2048]{2,1,0:T(8,128)(2,1)S(1)}, bf16[64,16,2048]{2,1,0:T(8,128)(2,1)}, u32[]{:S(2)}) %copy-start.3) | copy-done | bytes 4194328
  131.4 2.2 %copy-done.7 = bf16[64,16,2048]{2,1,0:T(8,128)(2,1)S(1)} copy-done((bf16[64,16,2048]{2,1,0:T(8,128)(2,1)S(1)}, bf16[64,16,2048]{2,1,0:T(8,128)(2,1)}, u32[]{:S(2)}) %copy-start.7) | copy-done | bytes 4194328
  133.6 5.6 %shard_map.74.refs_6_ = bf16[1024,2048]{1,0:T(8,128)(2,1)S(1)} custom-call(bf16[64,16,128]{2,1,0:T(8,128)(2,1)} %shard_map.73.refs_0_, bf16[64,16,128]{2,1,0:T(8,128)(2,1)} %collective-permute-done.3.refs_1_, bf16[1024,640]{1,0:T(8,128)(2,1)S(1)} %copy-done.10, bf16[64,16,2048]{2,1,0:T(8,128)(2,1)S(1)} %copy-done.3, bf16[64,16,2048]{2,1,0:T(8,128)(2,1)S(1)} %copy-done.7, ...), custom_call_target="tpu_custom_call" | custom-call | flops 3758096384 | bytes 16777216 | tf_op jit(solution)/shard_map/pallas_call | solution.py:151
  139.2 1.9 %collective-permute-done.2.mirror_ref = bf16[64,16,256]{2,1,0:T(8,128)(2,1)S(1)} collective-permute-done((bf16[64,16,256]{2,1,0:T(8,128)(2,1)S(1)}, bf16[64,16,256]{2,1,0:T(8,128)(2,1)S(1)}, u32[]{:S(2)}, u32[]{:S(2)}) %collective-permute-start.2) | collective-permute-done | bytes 524320 | tf_op jit(solution)/shard_map/ppermute | solution.py:16
  141.1 2.4 %shard_map.72.refs_5_ = bf16[256,2048]{1,0:T(8,128)(2,1)S(1)} custom-call(bf16[64,16,256]{2,1,0:T(8,128)(2,1)S(1)} %shard_map.71.own_ref, bf16[64,16,256]{2,1,0:T(8,128)(2,1)S(1)} %collective-permute-done.2.mirror_ref, bf16[64,16,2048]{2,1,0:T(8,128)(2,1)S(1)} %copy-done.3, bf16[64,16,2048]{2,1,0:T(8,128)(2,1)S(1)} %copy-done.7), custom_call_target="tpu_custom_call" | custom-call | flops 2147483648 | bytes 16777216 | tf_op jit(solution)/shard_map/pallas_call | solution.py:106
  143.4 1.2 collective-permute-done.1.refs_1_
  144.6 4.5 %shard_map.75 = bf16[1024,2048]{1,0:T(8,128)(2,1)} custom-call(bf16[64,16,128]{2,1,0:T(8,128)(2,1)S(1)} %shard_map.70.refs_0_, bf16[64,16,128]{2,1,0:T(8,128)(2,1)S(1)} %collective-permute-done.1.refs_1_, bf16[1024,384]{1,0:T(8,128)(2,1)S(1)} %compare_convert_fusion.1.refs_2_, bf16[64,16,2048]{2,1,0:T(8,128)(2,1)S(1)} %copy-done.4, ...), custom_call_target="tpu_custom_call" | custom-call | flops 2684354560 | bytes 16777216 | tf_op jit(solution)/shard_map/pallas_call | solution.py:151
  (41 shorter events, 5.2 us)
Async XLA Ops:
  0.0 1.7 %copy-start = (bf16[32,16,1024]{2,1,0:T(8,128)(2,1)S(1)}, bf16[32,16,1024]{2,1,0:T(8,128)(2,1)}, u32[]{:S(2)}) copy-start(bf16[32,16,1024]{2,1,0:T(8,128)(2,1)} %param.6) | copy-start | bytes 3145732
  3.7 1.5 %copy-start.8 = (bf16[128,16,640]{2,1,0:T(8,128)(2,1)}, bf16[128,16,640]{2,1,0:T(8,128)(2,1)S(1)}, u32[]{:S(2)}) copy-start(bf16[128,16,640]{2,1,0:T(8,128)(2,1)S(1)} %shard_map.67) | copy-start | bytes 7864324
  5.2 12.3 %copy-start.15 = (s32[64]{0:T(128)S(1)}, s32[64]{0:T(128)}, u32[]{:S(2)}) copy-start(s32[64]{0:T(128)} %param.11) | copy-start | bytes 772
  5.2 74.7 %all-to-all-start = ((bf16[128,16,640]{2,1,0:T(8,128)(2,1)}), bf16[128,16,640]{2,1,0:T(8,128)(2,1)}, u32[]{:S(2)}, u32[]{:S(2)}) async-start(bf16[128,16,640]{2,1,0:T(8,128)(2,1)} %copy-done.8), calls=%async_computation | async-start | bytes 5242880 | tf_op jit(solution)/shard_map/all_to_all | solution.py:220
  22.3 2.2 %copy-start.11 = (bf16[1,64,16,2048]{3,2,1,0:T(8,128)(2,1)S(1)}, bf16[1,64,16,2048]{3,2,1,0:T(8,128)(2,1)}, u32[]{:S(2)}) copy-start(bf16[1,64,16,2048]{3,2,1,0:T(8,128)(2,1)} %param.7) | copy-start | bytes 12582916
  24.5 3.7 %copy-start.12 = (bf16[1,64,16,2048]{3,2,1,0:T(8,128)(2,1)S(1)}, bf16[1,64,16,2048]{3,2,1,0:T(8,128)(2,1)}, u32[]{:S(2)}) copy-start(bf16[1,64,16,2048]{3,2,1,0:T(8,128)(2,1)} %param.8) | copy-start | bytes 12582916
  24.8 2.1 %copy-start.1 = (bf16[64,16,2048]{2,1,0:T(8,128)(2,1)}, bf16[64,16,2048]{2,1,0:T(8,128)(2,1)S(1)}, u32[]{:S(2)}) copy-start(bf16[64,16,2048]{2,1,0:T(8,128)(2,1)S(1)} %shard_map.64.plus_ref.refs_3_) | copy-start | bytes 12582916
  28.5 2.0 %copy-start.5 = (bf16[64,16,2048]{2,1,0:T(8,128)(2,1)}, bf16[64,16,2048]{2,1,0:T(8,128)(2,1)S(1)}, u32[]{:S(2)}) copy-start(bf16[64,16,2048]{2,1,0:T(8,128)(2,1)S(1)} %shard_map.65.minus_ref.refs_4_) | copy-start | bytes 12582916
  31.1 1.1 copy-start.9
  79.9 45.5 %all-to-all-start.1 = ((bf16[128,16,384]{2,1,0:T(8,128)(2,1)}), bf16[128,16,384]{2,1,0:T(8,128)(2,1)S(1)}, u32[]{:S(2)}, u32[]{:S(2)}) async-start(bf16[128,16,384]{2,1,0:T(8,128)(2,1)} %copy-done.9), calls=%async_computation.1 | async-start | bytes 3145728 | tf_op jit(solution)/shard_map/all_to_all | solution.py:227
  85.4 28.2 %copy-start.2 = (bf16[64,16,2048]{2,1,0:T(8,128)(2,1)S(1)}, bf16[64,16,2048]{2,1,0:T(8,128)(2,1)}, u32[]{:S(2)}) copy-start(bf16[64,16,2048]{2,1,0:T(8,128)(2,1)} %copy-done.1) | copy-start | bytes 12582916
  87.4 26.1 %collective-permute-start = (bf16[64,16,512]{2,1,0:T(8,128)(2,1)S(1)}, bf16[64,16,512]{2,1,0:T(8,128)(2,1)S(1)}, u32[]{:S(2)}, u32[]{:S(2)}) collective-permute-start(bf16[64,16,512]{2,1,0:T(8,128)(2,1)S(1)} %shard_map.68.own_ref), channel_id=1, source_target_pairs={{0,1},{1,0},{2,3},{3,2},{4,5},{5,4},{6,7},{7,6},{8,9},{9,8},{10,11... | collective-permute-start | bytes 3145736 | tf_op jit(solution)/shard_map/ppermute | solution.py:16
  90.4 38.8 %collective-permute-start.3 = (bf16[64,16,128]{2,1,0:T(8,128)(2,1)}, bf16[64,16,128]{2,1,0:T(8,128)(2,1)}, u32[]{:S(2)}, u32[]{:S(2)}) collective-permute-start(bf16[64,16,128]{2,1,0:T(8,128)(2,1)} %shard_map.73.refs_0_), channel_id=1, source_target_pairs={{0,1},{1,0},{2,3},{3,2},{4,5},{5,4},{6,7},{7,6},{8,9},{9,8},{10,11... | collective-permute-start | bytes 786440 | tf_op jit(solution)/shard_map/ppermute | solution.py:16
  113.5 2.2 %copy-start.6 = (bf16[64,16,2048]{2,1,0:T(8,128)(2,1)S(1)}, bf16[64,16,2048]{2,1,0:T(8,128)(2,1)}, u32[]{:S(2)}) copy-start(bf16[64,16,2048]{2,1,0:T(8,128)(2,1)} %copy-done.5) | copy-start | bytes 12582916
  120.3 1.4 copy-start.13
  125.4 3.8 %copy-start.10 = (bf16[1024,640]{1,0:T(8,128)(2,1)S(1)}, bf16[1024,640]{1,0:T(8,128)(2,1)}, u32[]{:S(2)}) copy-start(bf16[1024,640]{1,0:T(8,128)(2,1)} %compare_convert_fusion.refs_2_) | copy-start | bytes 3932164
  125.4 3.8 %copy-start.14 = (bf16[512,2048]{1,0:T(8,128)(2,1)S(1)}, bf16[512,2048]{1,0:T(8,128)(2,1)}, u32[]{:S(2)}) copy-start(bf16[512,2048]{1,0:T(8,128)(2,1)} %copy-done.13) | copy-start | bytes 6291460
  126.1 14.9 %collective-permute-start.2 = (bf16[64,16,256]{2,1,0:T(8,128)(2,1)S(1)}, bf16[64,16,256]{2,1,0:T(8,128)(2,1)S(1)}, u32[]{:S(2)}, u32[]{:S(2)}) collective-permute-start(bf16[64,16,256]{2,1,0:T(8,128)(2,1)S(1)} %shard_map.71.own_ref), channel_id=1, source_target_pairs={{0,1},{1,0},{2,3},{3,2},{4,5},{5,4},{6,7},{7,6},{8,9},{9,8},{10,11... | collective-permute-start | bytes 1572872 | tf_op jit(solution)/shard_map/ppermute | solution.py:16
  127.1 17.5 %collective-permute-start.1 = (bf16[64,16,128]{2,1,0:T(8,128)(2,1)S(1)}, bf16[64,16,128]{2,1,0:T(8,128)(2,1)S(1)}, u32[]{:S(2)}, u32[]{:S(2)}) collective-permute-start(bf16[64,16,128]{2,1,0:T(8,128)(2,1)S(1)} %shard_map.70.refs_0_), channel_id=1, source_target_pairs={{0,1},{1,0},{2,3},{3,2},{4,5},{5,4},{6,7},{7,6},{8,9},{9,8},{10,11... | collective-permute-start | bytes 786440 | tf_op jit(solution)/shard_map/ppermute | solution.py:16
  129.2 2.2 %copy-start.3 = (bf16[64,16,2048]{2,1,0:T(8,128)(2,1)S(1)}, bf16[64,16,2048]{2,1,0:T(8,128)(2,1)}, u32[]{:S(2)}) copy-start(bf16[64,16,2048]{2,1,0:T(8,128)(2,1)} %copy-done.1) | copy-start | bytes 12582916
  131.4 2.2 %copy-start.7 = (bf16[64,16,2048]{2,1,0:T(8,128)(2,1)S(1)}, bf16[64,16,2048]{2,1,0:T(8,128)(2,1)}, u32[]{:S(2)}) copy-start(bf16[64,16,2048]{2,1,0:T(8,128)(2,1)} %copy-done.5) | copy-start | bytes 12582916
  141.1 3.6 %copy-start.4 = (bf16[64,16,2048]{2,1,0:T(8,128)(2,1)S(1)}, bf16[64,16,2048]{2,1,0:T(8,128)(2,1)}, u32[]{:S(2)}) copy-start(bf16[64,16,2048]{2,1,0:T(8,128)(2,1)} %copy-done.1) | copy-start | bytes 12582916
